TPU v7x, 32 devices: a whole 2x2x4 slice. The times are simulated.
32 devices in a mesh: fsdp: 8 (over z, y), ctx: 4 (over x, core).
Axes of the slice: x: 2, y: 2, z: 4, core: 2. Of those that a mesh axis runs over, the one named last changes fastest.
Arguments:
- tokens: bfloat16 [16, 2048, 576], P('fsdp', 'ctx'), may hold values from -6 to 6
- cotangent: bfloat16 [16, 2048, 576], P('fsdp', 'ctx'), may hold values from -6 to 6
- span_order: int32 [8], replicated, may hold values from 0 to 7, each once
- norm_one: bfloat16 [576], P('fsdp'), may hold values from 0.5 to 1.5
- w_query: bfloat16 [576, 576], P('fsdp'), may hold values from -0.25 to 0.25
- w_key: bfloat16 [576, 192], P('fsdp'), may hold values from -0.25 to 0.25
- w_value: bfloat16 [576, 192], P('fsdp'), may hold values from -0.25 to 0.25
- w_out: bfloat16 [576, 576], P('fsdp'), may hold values from -1.5 to 1.5
- norm_two: bfloat16 [576], P('fsdp'), may hold values from 0.5 to 1.5
- w_gate: bfloat16 [576, 1536], P('fsdp'), may hold values from -0.25 to 0.25
- w_up: bfloat16 [576, 1536], P('fsdp'), may hold values from -0.25 to 0.25
- w_down: bfloat16 [1536, 576], P('fsdp'), may hold values from -0.15625 to 0.15625
Outputs:
- output: bfloat16 [16, 2048, 576], P('fsdp', 'ctx')
- grad_input: float32 [16, 2048, 576], P('fsdp', 'ctx')
- grad_norm_one: float32 [576], P('fsdp')
- grad_w_query: float32 [576, 576], P('fsdp')
- grad_w_key: float32 [576, 192], P('fsdp')
- grad_w_value: float32 [576, 192], P('fsdp')
- grad_w_out: float32 [576, 576], P('fsdp')
- grad_norm_two: float32 [576], P('fsdp')
- grad_w_gate: float32 [576, 1536], P('fsdp')
- grad_w_up: float32 [576, 1536], P('fsdp')
- grad_w_down: float32 [1536, 576], P('fsdp')
Inputs may be any that keep to these rules, and one draw needn't show every extreme that they name: `span_order`: every span number appears once.
All inputs are finite; a program needn't handle non-finite values.
Results may differ from a plain program's by a relative error of at most 0.015.
Values may be sent and summed in bfloat16 or wider, within the bound.
A program may use at most 384 MiB of HBM per device.

v0:
```python
import jax
import jax.numpy as jnp
from jax import lax
from jax.sharding import PartitionSpec as P

Q_HEADS = 9
KV_HEADS = 3
HEAD = 64


epsilon = 1e-05
rope_base = 100000.0


def rms_norm(values, gain_vector):
    scaling = lax.rsqrt(jnp.mean(values * values, axis=-1, keepdims=True) + epsilon)
    return values * scaling * gain_vector


def rotate(heads_in, positions):
    half_size = heads_in.shape[-1] // 2
    frequency = rope_base ** (-2.0 * jnp.arange(half_size, dtype=jnp.float32) / heads_in.shape[-1])
    angles = positions.astype(jnp.float32)[:, None] * frequency[None, :]
    cosine = jnp.cos(angles)[:, None, :]
    sine_part = jnp.sin(angles)[:, None, :]
    first_half = heads_in[..., :half_size]
    second_half = heads_in[..., half_size:]
    return jnp.concatenate(
        [
            first_half * cosine - second_half * sine_part,
            second_half * cosine + first_half * sine_part,
        ],
        axis=-1,
    )


def product(left_side, right_side, pattern):
    return jnp.einsum(pattern, left_side, right_side, preferred_element_type=jnp.float32)


def swish_gate(gate_in, upper_in):
    return jax.nn.silu(gate_in) * upper_in


def masked_scores(block_query, keys_seq, block_mask):
    scores = product(block_query, keys_seq, "qkgd,skd->kgqs")
    return jnp.where(block_mask[None, None], scores, -1e30)


def forward_block(block_query, keys_seq, values_seq, block_mask):
    scores = masked_scores(block_query, keys_seq, block_mask)
    topmost = jnp.max(scores, axis=-1, keepdims=True)
    raised = jnp.exp(scores - topmost)
    totals = jnp.sum(raised, axis=-1, keepdims=True)
    weights = (raised / totals).astype(jnp.bfloat16)
    mixed = product(weights, values_seq, "kgqs,skd->qkgd")
    return (mixed, (topmost + jnp.log(totals))[..., 0])


def backward_block(block_query, block_grad, block_total, keys_seq, values_seq, block_mask):
    scores = masked_scores(block_query, keys_seq, block_mask)
    probability = jnp.exp(scores - block_total[..., None])
    grad_probability = product(block_grad, values_seq, "qkgd,skd->kgqs")
    inner_sum = jnp.sum(probability * grad_probability, axis=-1, keepdims=True)
    grad_scores = (probability * (grad_probability - inner_sum)).astype(jnp.bfloat16)
    return (probability, grad_scores, inner_sum[..., 0])


def body(
    tokens,
    cotangent,
    span_order,
    norm_one,
    w_query,
    w_key,
    w_value,
    w_out,
    norm_two,
    w_gate,
    w_up,
    w_down,
):
    sequences, local_rows, model_width = tokens.shape
    context_size = lax.axis_size("ctx")
    span_size = local_rows // 2
    full_rows = local_rows * context_size
    group_size = Q_HEADS // KV_HEADS
    key_width = KV_HEADS * HEAD
    query_width = Q_HEADS * HEAD
    token_count = sequences * local_rows
    all_places = (
        span_order[:, None] * span_size + jnp.arange(span_size, dtype=jnp.int32)[None, :]
    ).reshape(full_rows)
    own_places = lax.dynamic_slice_in_dim(
        all_places, lax.axis_index("ctx") * local_rows, local_rows
    )
    row_places = jnp.tile(own_places, sequences)
    allowed = (own_places[:, None] >= all_places[None, :]).reshape(2, span_size, full_rows)
    gain_one, query_matrix, key_matrix, value_matrix, out_matrix = (
        lax.all_gather(norm_one, "fsdp", axis=0, tiled=True),
        lax.all_gather(w_query, "fsdp", axis=0, tiled=True),
        lax.all_gather(w_key, "fsdp", axis=0, tiled=True),
        lax.all_gather(w_value, "fsdp", axis=0, tiled=True),
        lax.all_gather(w_out, "fsdp", axis=0, tiled=True),
    )
    hidden_in = tokens.reshape(token_count, model_width).astype(jnp.float32)
    normed = rms_norm(hidden_in, gain_one.astype(jnp.float32)).astype(jnp.bfloat16)
    query_pre = jnp.dot(normed, query_matrix, preferred_element_type=jnp.float32)
    key_pre = jnp.dot(normed, key_matrix, preferred_element_type=jnp.float32)
    value_pre = jnp.dot(normed, value_matrix, preferred_element_type=jnp.float32)

    def query_rope(raw_heads):
        return rotate(raw_heads.reshape(token_count, Q_HEADS, HEAD), row_places) * 0.125

    def key_rope(raw_heads):
        return rotate(raw_heads.reshape(token_count, KV_HEADS, HEAD), row_places)

    queries = query_rope(query_pre).astype(jnp.bfloat16)
    keys_own = key_rope(key_pre).astype(jnp.bfloat16).reshape(sequences, local_rows, key_width)
    values_own = value_pre.astype(jnp.bfloat16).reshape(sequences, local_rows, key_width)
    keys_every, values_every = (
        lax.all_gather(keys_own, "ctx", axis=1, tiled=True),
        lax.all_gather(values_own, "ctx", axis=1, tiled=True),
    )
    keys_seqs = keys_every.reshape(sequences, full_rows, KV_HEADS, HEAD)
    values_seqs = values_every.reshape(sequences, full_rows, KV_HEADS, HEAD)
    query_blocks = queries.reshape(sequences, 2, span_size, KV_HEADS, group_size, HEAD)

    def attend_sequence(inputs_set):
        seq_query, keys_seq, values_seq = inputs_set

        def attend_one_block(pair):
            return forward_block(pair[0], keys_seq, values_seq, pair[1])

        return lax.map(attend_one_block, (seq_query, allowed))

    mixed_heads, log_total = lax.map(attend_sequence, (query_blocks, keys_seqs, values_seqs))
    attended = mixed_heads.reshape(token_count, query_width).astype(jnp.bfloat16)
    middle = hidden_in + jnp.dot(attended, out_matrix, preferred_element_type=jnp.float32)
    gain_two, gate_matrix, up_matrix, down_matrix = (
        lax.all_gather(norm_two, "fsdp", axis=0, tiled=True),
        lax.all_gather(w_gate, "fsdp", axis=0, tiled=True),
        lax.all_gather(w_up, "fsdp", axis=0, tiled=True),
        lax.all_gather(w_down, "fsdp", axis=0, tiled=True),
    )
    normed_two = rms_norm(middle, gain_two.astype(jnp.float32)).astype(jnp.bfloat16)
    gate_pre = jnp.dot(normed_two, gate_matrix, preferred_element_type=jnp.float32)
    up_pre = jnp.dot(normed_two, up_matrix, preferred_element_type=jnp.float32)
    inner_act = swish_gate(gate_pre, up_pre).astype(jnp.bfloat16)
    output = middle + jnp.dot(inner_act, down_matrix, preferred_element_type=jnp.float32)
    back_attn = (
        lax.all_gather(norm_one, "fsdp", axis=0, tiled=True),
        lax.all_gather(w_query, "fsdp", axis=0, tiled=True),
        lax.all_gather(w_key, "fsdp", axis=0, tiled=True),
        lax.all_gather(w_value, "fsdp", axis=0, tiled=True),
        lax.all_gather(w_out, "fsdp", axis=0, tiled=True),
    )
    back_mlp = (
        lax.all_gather(norm_two, "fsdp", axis=0, tiled=True),
        lax.all_gather(w_gate, "fsdp", axis=0, tiled=True),
        lax.all_gather(w_up, "fsdp", axis=0, tiled=True),
        lax.all_gather(w_down, "fsdp", axis=0, tiled=True),
    )
    back_gain_one, back_query, back_key, back_value, back_out = back_attn
    back_gain_two, back_gate, back_up, back_down = back_mlp
    upstream = cotangent.reshape(token_count, model_width).astype(jnp.float32)
    upstream_low = upstream.astype(jnp.bfloat16)
    grad_down = product(inner_act, upstream_low, "nf,nd->fd")
    grad_inner = product(upstream_low, back_down, "nd,fd->nf")
    _, inner_pull = jax.vjp(swish_gate, gate_pre, up_pre)
    grad_gate_pre, grad_up_pre = inner_pull(grad_inner)
    gate_low = grad_gate_pre.astype(jnp.bfloat16)
    upper_low = grad_up_pre.astype(jnp.bfloat16)
    grad_gate = product(normed_two, gate_low, "nd,nf->df")
    grad_up = product(normed_two, upper_low, "nd,nf->df")
    grad_normed_two = product(gate_low, back_gate, "nf,df->nd") + product(
        upper_low, back_up, "nf,df->nd"
    )
    _, second_pull = jax.vjp(rms_norm, middle, back_gain_two.astype(jnp.float32))
    grad_middle_norm, grad_gain_two = second_pull(grad_normed_two)
    grad_middle = upstream + grad_middle_norm
    middle_low = grad_middle.astype(jnp.bfloat16)
    grad_out = product(attended, middle_low, "nh,nd->hd")
    grad_attended = product(middle_low, back_out, "nd,hd->nh").astype(jnp.bfloat16)
    grad_blocks = grad_attended.reshape(sequences, 2, span_size, KV_HEADS, group_size, HEAD)

    def back_sequence(inputs_set):
        seq_query, seq_grad, seq_total, keys_seq, values_seq = inputs_set

        def back_one_block(carry, pieces):
            key_sum, value_sum = carry
            block_query, block_grad, block_total, block_mask = pieces
            probability, grad_scores, _ = backward_block(
                block_query, block_grad, block_total, keys_seq, values_seq, block_mask
            )
            query_grad = product(grad_scores, keys_seq, "kgqs,skd->qkgd")
            key_sum = key_sum + product(grad_scores, block_query, "kgqs,qkgd->skd")
            value_sum = value_sum + product(
                probability.astype(jnp.bfloat16), block_grad, "kgqs,qkgd->skd"
            )
            return ((key_sum, value_sum), query_grad)

        empty = jnp.zeros((full_rows, KV_HEADS, HEAD), jnp.float32)
        sums, query_grad = lax.scan(
            back_one_block, (empty, empty), (seq_query, seq_grad, seq_total, allowed)
        )
        return (query_grad, sums[0], sums[1])

    query_grads, key_grads, value_grads = lax.map(
        back_sequence, (query_blocks, grad_blocks, log_total, keys_seqs, values_seqs)
    )
    key_part, value_part = (
        lax.psum_scatter(
            key_grads.reshape(sequences, full_rows, key_width),
            "ctx",
            scatter_dimension=1,
            tiled=True,
        ),
        lax.psum_scatter(
            value_grads.reshape(sequences, full_rows, key_width),
            "ctx",
            scatter_dimension=1,
            tiled=True,
        ),
    )
    key_mine = key_part.reshape(token_count, key_width)
    value_mine = value_part.reshape(token_count, key_width)
    _, query_pull = jax.vjp(query_rope, query_pre)
    query_low = query_pull(query_grads.reshape(token_count, Q_HEADS, HEAD))[0].astype(jnp.bfloat16)
    _, key_pull = jax.vjp(key_rope, key_pre)
    key_low = key_pull(key_mine.reshape(token_count, KV_HEADS, HEAD))[0].astype(jnp.bfloat16)
    value_low = value_mine.astype(jnp.bfloat16)
    grad_query = product(normed, query_low, "nd,nh->dh")
    grad_key = product(normed, key_low, "nd,nh->dh")
    grad_value = product(normed, value_low, "nd,nh->dh")
    grad_normed = (
        product(query_low, back_query, "nh,dh->nd")
        + product(key_low, back_key, "nh,dh->nd")
        + product(value_low, back_value, "nh,dh->nd")
    )
    _, first_pull = jax.vjp(rms_norm, hidden_in, back_gain_one.astype(jnp.float32))
    grad_hidden_norm, grad_gain_one = first_pull(grad_normed)
    grad_input = grad_middle + grad_hidden_norm
    attn_parts = (
        lax.psum_scatter(grad_gain_one, "fsdp", scatter_dimension=0, tiled=True),
        lax.psum_scatter(grad_query, "fsdp", scatter_dimension=0, tiled=True),
        lax.psum_scatter(grad_key, "fsdp", scatter_dimension=0, tiled=True),
        lax.psum_scatter(grad_value, "fsdp", scatter_dimension=0, tiled=True),
        lax.psum_scatter(grad_out, "fsdp", scatter_dimension=0, tiled=True),
    )
    mlp_parts = (
        lax.psum_scatter(grad_gain_two, "fsdp", scatter_dimension=0, tiled=True),
        lax.psum_scatter(grad_gate, "fsdp", scatter_dimension=0, tiled=True),
        lax.psum_scatter(grad_up, "fsdp", scatter_dimension=0, tiled=True),
        lax.psum_scatter(grad_down, "fsdp", scatter_dimension=0, tiled=True),
    )
    summed = (
        lax.psum(attn_parts[0].astype(jnp.bfloat16), "ctx").astype(jnp.float32),
        lax.psum(attn_parts[1].astype(jnp.bfloat16), "ctx").astype(jnp.float32),
        lax.psum(attn_parts[2].astype(jnp.bfloat16), "ctx").astype(jnp.float32),
        lax.psum(attn_parts[3].astype(jnp.bfloat16), "ctx").astype(jnp.float32),
        lax.psum(attn_parts[4].astype(jnp.bfloat16), "ctx").astype(jnp.float32),
        lax.psum(mlp_parts[0].astype(jnp.bfloat16), "ctx").astype(jnp.float32),
        lax.psum(mlp_parts[1].astype(jnp.bfloat16), "ctx").astype(jnp.float32),
        lax.psum(mlp_parts[2].astype(jnp.bfloat16), "ctx").astype(jnp.float32),
        lax.psum(mlp_parts[3].astype(jnp.bfloat16), "ctx").astype(jnp.float32),
    )
    return (
        output.astype(jnp.bfloat16).reshape(tokens.shape),
        grad_input.reshape(tokens.shape),
        summed[0],
        summed[1],
        summed[2],
        summed[3],
        summed[4],
        summed[5],
        summed[6],
        summed[7],
        summed[8],
    )


def solution(mesh):
    in_specs = (
        P("fsdp", "ctx", None),
        P("fsdp", "ctx", None),
        P(),
        P("fsdp"),
        P("fsdp", None),
        P("fsdp", None),
        P("fsdp", None),
        P("fsdp", None),
        P("fsdp"),
        P("fsdp", None),
        P("fsdp", None),
        P("fsdp", None),
    )
    out_specs = (
        P("fsdp", "ctx", None),
        P("fsdp", "ctx", None),
        P("fsdp"),
        P("fsdp", None),
        P("fsdp", None),
        P("fsdp", None),
        P("fsdp", None),
        P("fsdp"),
        P("fsdp", None),
        P("fsdp", None),
        P("fsdp", None),
    )
    return jax.shard_map(body, mesh=mesh, in_specs=in_specs, out_specs=out_specs, check_vma=False)
```

profile of v0, /device:TPU:0, one launch (start us, length us, event | category | flops | bytes accessed | tf_op | source)
XLA Modules:
  0.0 1666.9 jit_solution(9202660116636979222)
XLA Ops:
  12.1 23.7 %all-reduce.11 = (bf16[576]{0:T(1024)(128)(2,1)S(1)}, bf16[576]{0:T(1024)(128)(2,1)}) all-reduce(bf16[576]{0:T(1024)(128)(2,1)S(1)} %dynamic-update-slice, bf16[576]{0:T(1024)(128)(2,1)S(1)} %dynamic-update-slice.1), channel_id=1, replica_groups=mesh['fsdp'=8,'ctx'=4] {'fsdp'}, use_global_device_ids=true, to_apply=%add.4 | all-reduce | flops 1152 | bytes 4608
  38.7 31.0 %all_gather.44 = bf16[576,192]{1,0:T(8,128)(2,1)S(1)} all-gather(bf16[72,192]{1,0:T(8,128)(2,1)} %param.25), channel_id=1, replica_groups=mesh['fsdp'=8,'ctx'=4] {'fsdp'}, dimensions={0}, use_global_device_ids=true | all-gather | bytes 248832 | tf_op jit(solution)/shard_map/all_gather | solution.py:102
  79.1 30.9 %all_gather.46 = bf16[576,192]{1,0:T(8,128)(2,1)S(1)} all-gather(bf16[72,192]{1,0:T(8,128)(2,1)S(1)} %copy-done.65), channel_id=1, replica_groups=mesh['fsdp'=8,'ctx'=4] {'fsdp'}, dimensions={0}, use_global_device_ids=true | all-gather | bytes 248832 | tf_op jit(solution)/shard_map/all_gather | solution.py:103
  116.2 32.9 %all_gather.43 = bf16[576,576]{1,0:T(8,128)(2,1)S(1)} all-gather(bf16[72,576]{1,0:T(8,128)(2,1)S(1)} %copy-done.56), channel_id=1, replica_groups=mesh['fsdp'=8,'ctx'=4] {'fsdp'}, dimensions={0}, use_global_device_ids=true | all-gather | bytes 746496 | tf_op jit(solution)/shard_map/all_gather | solution.py:101
  149.0 35.4 %all_gather.48 = bf16[576,576]{1,0:T(8,128)(2,1)} all-gather(bf16[72,576]{1,0:T(8,128)(2,1)S(1)} %copy-done.57), channel_id=1, replica_groups=mesh['fsdp'=8,'ctx'=4] {'fsdp'}, dimensions={0}, use_global_device_ids=true | all-gather | bytes 746496 | tf_op jit(solution)/shard_map/all_gather | solution.py:104
  198.8 129.4 %while.64 = (s32[]{:T(128)}, bf16[2,2,256,3,3,64]{2,5,4,3,1,0:T(8,128)(2,1)}, f32[2,2,3,3,256]{4,3,2,1,0:T(4,128)}, bf16[2,2,256,3,3,64]{2,5,4,3,1,0:T(8,128)(2,...) while((s32[]{:T(128)}, ...), condition=%wide.region_6.7_spmd.clone.clone, body=%wide.region_1.6_spmd.clone.sunk.clone | while | flops 1251473152 | bytes 68474272 | solution.py:137
  203.2 58.0 %while.63 = (s32[]{:T(128)}, bf16[2,256,3,3,64]{1,4,3,2,0:T(8,128)(2,1)}, f32[2,3,3,256]{3,2,1,0:T(4,128)S(1)}, pred[2,256,2048]{2,1,0:T(8,128)(4,1)S(1)}, bf16[...) while((s32[]{:T(128)}, ...), condition=%wide.region_5.5_spmd, body=%wide.region_2.4_spmd.sunk | while | flops 1250424576 | bytes 61785196 | solution.py:135
  268.0 57.7 %while.63 = (s32[]{:T(128)}, bf16[2,256,3,3,64]{1,4,3,2,0:T(8,128)(2,1)}, f32[2,3,3,256]{3,2,1,0:T(4,128)S(1)}, pred[2,256,2048]{2,1,0:T(8,128)(4,1)S(1)}, bf16[...) while((s32[]{:T(128)}, ...), condition=%wide.region_5.5_spmd, body=%wide.region_2.4_spmd.sunk | while | flops 1250424576 | bytes 61785196 | solution.py:135
  374.7 340.9 %while.66 = (s32[]{:T(128)}, f32[2,2,256,3,3,64]{2,5,4,3,1,0:T(8,128)}, f32[2,2048,3,64]{1,0,3,2:T(2,128)}, f32[2,2048,3,64]{1,0,3,2:T(2,128)}, bf16[2,2,256,3,3...) while((s32[]{:T(128)}, ...), condition=%wide.region_13.14_spmd.clone.clone, body=%wide.region_9.13_spmd.clone.sunk.clone | while | flops 3079141120 | bytes 293599008 | solution.py:209
  384.1 100.8 %while.65 = (s32[]{:T(128)}, f32[2048,3,64]{0,2,1:T(8,128)S(1)}, f32[2048,3,64]{0,2,1:T(8,128)}, f32[2,256,3,3,64]{1,4,3,2,0:T(8,128)}, bf16[2,256,3,3,64]{1,4,3...) while((s32[]{:T(128)}, f32[2048,3,64]{0,2,1:T(8,128)S(1)}, ...), condition=%wide.region_12.12_spmd.clone, body=%wide.region_10.11_spmd.clone.sunk | while | flops 3078092544 | bytes 253492592 | solution.py:204
  415.4 13.8 fusion.151
  466.0 13.8 fusion.151
  489.5 26.9 %dynamic_update_slice.60 = f32[2,2048,3,64]{1,0,3,2:T(2,128)} dynamic-update-slice(f32[2,2048,3,64]{1,0,3,2:T(2,128)} %get-tuple-element.941, f32[1,2048,3,64]{1,0,3,2:T(1,128)S(1)} %copy-done.5, s32[]{:T(128)S(6)} %copy.164, s32[]{:T(128)} %constant.99.clone.1..sunk.4, s32[]{:T(128)} %constant.99.clone.1..sunk.4, s32[]{:T(128)} %constant.99.clone.1..sunk.4) | dynamic-update-slice | bytes 3145732 | tf_op jit(solution)/shard_map/while/body/jit(dynamic_update_index_in_dim)/dynamic_update_slice | solution.py:209
  518.1 27.0 %dynamic_update_slice.61 = f32[2,2048,3,64]{1,0,3,2:T(2,128)} dynamic-update-slice(f32[2,2048,3,64]{1,0,3,2:T(2,128)} %get-tuple-element.942, f32[1,2048,3,64]{1,0,3,2:T(1,128)S(1)} %copy.119, s32[]{:T(128)S(6)} %copy.164, s32[]{:T(128)} %constant.99.clone.1..sunk.4, s32[]{:T(128)} %constant.99.clone.1..sunk.4, s32[]{:T(128)} %constant.99.clone.1..sunk.4) | dynamic-update-slice | bytes 3145732 | tf_op jit(solution)/shard_map/while/body/jit(dynamic_update_index_in_dim)/dynamic_update_slice | solution.py:209
  554.3 100.8 %while.65 = (s32[]{:T(128)}, f32[2048,3,64]{0,2,1:T(8,128)S(1)}, f32[2048,3,64]{0,2,1:T(8,128)}, f32[2,256,3,3,64]{1,4,3,2,0:T(8,128)}, bf16[2,256,3,3,64]{1,4,3...) while((s32[]{:T(128)}, f32[2048,3,64]{0,2,1:T(8,128)S(1)}, ...), condition=%wide.region_12.12_spmd.clone, body=%wide.region_10.11_spmd.clone.sunk | while | flops 3078092544 | bytes 253492592 | solution.py:204
  585.5 13.8 fusion.151
  636.2 13.8 fusion.151
  659.7 26.9 %dynamic_update_slice.60 = f32[2,2048,3,64]{1,0,3,2:T(2,128)} dynamic-update-slice(f32[2,2048,3,64]{1,0,3,2:T(2,128)} %get-tuple-element.941, f32[1,2048,3,64]{1,0,3,2:T(1,128)S(1)} %copy-done.5, s32[]{:T(128)S(6)} %copy.164, s32[]{:T(128)} %constant.99.clone.1..sunk.4, s32[]{:T(128)} %constant.99.clone.1..sunk.4, s32[]{:T(128)} %constant.99.clone.1..sunk.4) | dynamic-update-slice | bytes 3145732 | tf_op jit(solution)/shard_map/while/body/jit(dynamic_update_index_in_dim)/dynamic_update_slice | solution.py:209
  688.3 27.0 %dynamic_update_slice.61 = f32[2,2048,3,64]{1,0,3,2:T(2,128)} dynamic-update-slice(f32[2,2048,3,64]{1,0,3,2:T(2,128)} %get-tuple-element.942, f32[1,2048,3,64]{1,0,3,2:T(1,128)S(1)} %copy.119, s32[]{:T(128)S(6)} %copy.164, s32[]{:T(128)} %constant.99.clone.1..sunk.4, s32[]{:T(128)} %constant.99.clone.1..sunk.4, s32[]{:T(128)} %constant.99.clone.1..sunk.4) | dynamic-update-slice | bytes 3145732 | tf_op jit(solution)/shard_map/while/body/jit(dynamic_update_index_in_dim)/dynamic_update_slice | solution.py:209
  715.7 95.1 %copy.78 = f32[2,2048,192]{0,2,1:T(8,128)} copy(f32[2,2048,192]{1,0,2:T(2,128)} %bitcast.350) | data formatting | bytes 6291456
  810.7 134.7 %reshape.326 = f32[2048,384]{1,0:T(8,128)} reshape(f32[2048,192,2]{2,1,0:T(8,128)} %bitcast.58) | data formatting | bytes 6291456
  964.7 95.1 %copy.76 = f32[2,2048,192]{0,2,1:T(8,128)} copy(f32[2,2048,192]{1,0,2:T(2,128)} %bitcast.351) | data formatting | bytes 6291456
  1059.8 135.0 %reshape.324 = f32[2048,384]{1,0:T(8,128)} reshape(f32[2048,192,2]{2,1,0:T(8,128)} %bitcast.55) | data formatting | bytes 6291456
  1223.1 54.9 %reshape.327 = bf16[512,192,2]{2,1,0:T(8,128)(2,1)} reshape(f32[512,384]{1,0:T(8,128)} %reduce-scatter.30.cloned.1.call-done) | data formatting | bytes 1179648
  1278.0 23.7 %copy.79 = bf16[2,512,192]{1,0,2:T(2,128)(2,1)S(1)} copy(bf16[2,512,192]{0,2,1:T(8,128)(2,1)} %bitcast.334) | data formatting | bytes 786432
  1309.8 52.5 %reshape.325 = f32[512,192,2]{2,1,0:T(8,128)} reshape(f32[512,384]{1,0:T(8,128)} %reduce-scatter.28.cloned.1.call-done) | data formatting | bytes 1572864
  1362.3 28.1 %copy.77 = f32[2,512,192]{1,0,2:T(2,128)S(1)} copy(f32[2,512,192]{0,2,1:T(8,128)} %bitcast.333) | data formatting | bytes 1572864
  1399.0 18.7 %all-reduce.10 = (bf16[576]{0:T(1024)(128)(2,1)S(1)}, bf16[576]{0:T(1024)(128)(2,1)S(1)}) all-reduce(f32[576]{0:T(1024)S(1)} %get-tuple-element.362, f32[576]{0:T(1024)S(1)} %copy-done.70), channel_id=4, replica_groups=mesh['fsdp'=8,'ctx'=4] {'fsdp'}, use_global_device_ids=true, to_apply=%region_18.19.clone | all-reduce | flops 1152 | bytes 6912
  1421.3 62.8 %reduce-scatter.24.cloned.1.call-done = f32[72,1536]{1,0:T(8,128)} async-done(((f32[576,1536]{1,0:T(8,128)}), f32[72,1536]{1,0:T(8,128)}) %reduce-scatter.24.cloned.1.call-update) | async-done | bytes 442384 | tf_op jit(solution)/shard_map/reduce_scatter | solution.py:254
  1490.4 59.0 %reduce-scatter.20.cloned.1.call-done = f32[72,192]{1,0:T(8,128)} async-done(((f32[576,192]{1,0:T(8,128)}), f32[72,192]{1,0:T(8,128)}) %reduce-scatter.20.cloned.1.call-update) | async-done | bytes 55312 | tf_op jit(solution)/shard_map/reduce_scatter | solution.py:248
  1550.4 63.4 %reduce-scatter.18.cloned.1.call-done = f32[72,192]{1,0:T(8,128)} async-done(((f32[576,192]{1,0:T(8,128)}), f32[72,192]{1,0:T(8,128)}) %reduce-scatter.18.cloned.1.call-update) | async-done | bytes 55312 | tf_op jit(solution)/shard_map/reduce_scatter | solution.py:247
  1628.7 23.1 %all-reduce.16.cloned.1.call-done = (bf16[72,576]{1,0:T(8,128)(2,1)}, bf16[72,576]{1,0:T(8,128)(2,1)}, bf16[72,1536]{1,0:T(8,128)(2,1)}, bf16[72,1536]{1,0:T(8,128)(2,1)}, bf16[192,576]{1,0:T(8,128)(2,1)}) async-done(((bf16[72,576]{1,0:T(8,128)(2,1)}, bf16[72,576]{1,0:T(8,128)(2,1)}, bf16[72,1536]{1,0:T(8,128)(2,1)}, bf16[72,1536]{1,0:T(8,128)(2,1)}, bf16[192,576]{1,0:T(8,128)(2,1)}), ...) | async-done | bytes 829456 | tf_op jit(solution)/shard_map/psum | solution.py:259
  (448 shorter events, 485.9 us)
Async XLA Ops:
  7.2 63.3 %copy-start.18 = (bf16[2,512,576]{1,2,0:T(8,128)(2,1)S(1)}, bf16[2,512,576]{1,2,0:T(8,128)(2,1)}, u32[]{:S(2)}) copy-start(bf16[2,512,576]{1,2,0:T(8,128)(2,1)} %param.20) | copy-start | bytes 3538948
  7.2 185.2 %all-gather.6.cloned.1.call-start = ((), (), s32[]{:S(2)}) async-start(), calls=%async_computation.9 | async-start | bytes 1966080 | tf_op jit(solution)/shard_map/all_gather | solution.py:122
  35.8 74.2 %copy-start.53 = (f32[576]{0:T(1024)}, f32[576]{0:T(1024)S(1)}, u32[]{:S(2)}) copy-start(f32[576]{0:T(1024)S(1)} %convert_element_type.178) | copy-start | bytes 6916
  37.9 32.9 %copy-start.60 = (f32[2,512]{1,0:T(2,128)}, f32[2,512]{1,0:T(2,128)S(1)}, u32[]{:S(2)}) copy-start(f32[2,512]{1,0:T(2,128)S(1)} %get-tuple-element.475) | copy-start | bytes 12292
  75.2 110.7 %copy-start.27 = (f32[1024,32]{0,1:T(8,128)}, f32[1024,32]{0,1:T(8,128)S(1)}, u32[]{:S(2)}) copy-start(f32[1024,32]{0,1:T(8,128)S(1)} %get-tuple-element.472) | copy-start | bytes 393220
  75.2 110.7 %copy-start.29 = (f32[1024,32]{0,1:T(8,128)}, f32[1024,32]{0,1:T(8,128)S(1)}, u32[]{:S(2)}) copy-start(f32[1024,32]{0,1:T(8,128)S(1)} %get-tuple-element.473) | copy-start | bytes 393220
  77.9 117.7 %all-gather.8.cloned.1.call-start = ((), (), s32[]{:S(2)}) async-start(), calls=%async_computation.10 | async-start | bytes 1966080 | tf_op jit(solution)/shard_map/all_gather | solution.py:123
  78.0 32.0 %copy-start.58 = (f32[1024]{0:T(1024)}, f32[1024]{0:T(1024)S(1)}, u32[]{:S(2)}) copy-start(f32[1024]{0:T(1024)S(1)} %rsqrt.26) | copy-start | bytes 12292
  79.1 30.9 %copy-start.6 = (f32[2,72,8,512]{3,2,0,1:T(8,128)}, f32[2,72,8,512]{3,2,0,1:T(8,128)S(1)}, u32[]{:S(2)}) copy-start(f32[2,72,8,512]{3,2,0,1:T(8,128)S(1)} %copy.97) | copy-start | bytes 7077892
  111.4 37.6 %copy-start.57 = (bf16[72,576]{1,0:T(8,128)(2,1)S(1)}, bf16[72,576]{1,0:T(8,128)(2,1)}, u32[]{:S(2)}) copy-start(bf16[72,576]{1,0:T(8,128)(2,1)} %param.27) | copy-start | bytes 248836
  112.4 227.5 %all-gather.12.cloned.1.call-start = ((), (), s32[]{:S(2)}) async-start(), calls=%async_computation.12 | async-start | bytes 1990656 | tf_op jit(solution)/shard_map/all_gather | solution.py:143
  113.2 233.3 %all-gather.10.cloned.1.call-start = ((), (), s32[]{:S(2)}) async-start(), calls=%async_computation.11 | async-start | bytes 1990656 | tf_op jit(solution)/shard_map/all_gather | solution.py:142
  113.8 238.8 %all-gather.14.cloned.1.call-start = ((), (), s32[]{:S(2)}) async-start(), calls=%async_computation.13 | async-start | bytes 2211840 | tf_op jit(solution)/shard_map/all_gather | solution.py:144
  114.4 1108.8 %reduce-scatter.30.cloned.1.call-start = ((), (), s32[]{:S(2)}) async-start(), calls=%async_computation.20 | async-start | bytes 3932160
  149.0 35.8 %copy-start.31 = (bf16[576,576]{1,0:T(8,128)(2,1)}, bf16[576,576]{1,0:T(8,128)(2,1)S(1)}, u32[]{:S(2)}) copy-start(bf16[576,576]{1,0:T(8,128)(2,1)S(1)} %all_gather.43) | copy-start | bytes 1990660
  203.2 60.5 %copy-start.46 = (s32[2048]{0:T(1024)S(1)}, s32[2048]{0:T(1024)}, u32[]{:S(2)}) copy-start(s32[2048]{0:T(1024)} %copy-done.45) | copy-start | bytes 24580 | tf_op jit(solution)/shard_map/while
  203.2 60.5 %copy-start.50 = (s32[2,256]{1,0:T(2,128)S(1)}, s32[2,256]{1,0:T(2,128)}, u32[]{:S(2)}) copy-start(s32[2,256]{1,0:T(2,128)} %copy-done.49) | copy-start | bytes 6148 | tf_op jit(solution)/shard_map/while
  268.0 60.3 %copy-start.46 = (s32[2048]{0:T(1024)S(1)}, s32[2048]{0:T(1024)}, u32[]{:S(2)}) copy-start(s32[2048]{0:T(1024)} %copy-done.45) | copy-start | bytes 24580 | tf_op jit(solution)/shard_map/while
  268.0 60.3 %copy-start.50 = (s32[2,256]{1,0:T(2,128)S(1)}, s32[2,256]{1,0:T(2,128)}, u32[]{:S(2)}) copy-start(s32[2,256]{1,0:T(2,128)} %copy-done.49) | copy-start | bytes 6148 | tf_op jit(solution)/shard_map/while
  487.7 28.8 %copy-start.9 = (f32[2048,3,64]{0,2,1:T(8,128)S(1)}, f32[2048,3,64]{0,2,1:T(8,128)}, u32[]{:S(2)}) copy-start(f32[2048,3,64]{0,2,1:T(8,128)} %get-tuple-element.815) | copy-start | bytes 4718596 | tf_op jit(solution)/shard_map/while
  657.9 28.8 %copy-start.9 = (f32[2048,3,64]{0,2,1:T(8,128)S(1)}, f32[2048,3,64]{0,2,1:T(8,128)}, u32[]{:S(2)}) copy-start(f32[2048,3,64]{0,2,1:T(8,128)} %get-tuple-element.815) | copy-start | bytes 4718596 | tf_op jit(solution)/shard_map/while
  945.5 360.4 %reduce-scatter.34.cloned.1.call-start = ((), (), s32[]{:S(2)}) async-start(), calls=%async_computation.22 | async-start | bytes 1658880
  950.6 356.8 %reduce-scatter.32.cloned.1.call-start = ((), (), s32[]{:S(2)}) async-start(), calls=%async_computation.21 | async-start | bytes 1658880
  964.7 345.1 %reduce-scatter.28.cloned.1.call-start = ((), (), s32[]{:S(2)}) async-start(), calls=%async_computation.19 | async-start | bytes 3932160
  1194.8 223.0 %reduce-scatter.26.cloned.1.call-start = ((), (), s32[]{:S(2)}) async-start(), calls=%async_computation.18 | async-start | bytes 4423680 | tf_op jit(solution)/shard_map/reduce_scatter | solution.py:255
  1202.6 217.0 %reduce-scatter.22.cloned.1.call-start = ((), (), s32[]{:S(2)}) async-start(), calls=%async_computation.16 | async-start | bytes 3981312 | tf_op jit(solution)/shard_map/reduce_scatter | solution.py:253
  1209.6 274.5 %reduce-scatter.24.cloned.1.call-start = ((), (), s32[]{:S(2)}) async-start(), calls=%async_computation.17 | async-start | bytes 3981312 | tf_op jit(solution)/shard_map/reduce_scatter | solution.py:254
  1215.8 333.7 %reduce-scatter.20.cloned.1.call-start = ((), (), s32[]{:S(2)}) async-start(), calls=%async_computation.15 | async-start | bytes 663552 | tf_op jit(solution)/shard_map/reduce_scatter | solution.py:248
  1303.1 310.7 %reduce-scatter.18.cloned.1.call-start = ((), (), s32[]{:S(2)}) async-start(), calls=%async_computation.14 | async-start | bytes 663552 | tf_op jit(solution)/shard_map/reduce_scatter | solution.py:247
  1362.3 28.8 %copy-start.28 = (f32[1024,32]{0,1:T(8,128)S(1)}, f32[1024,32]{0,1:T(8,128)}, u32[]{:S(2)}) copy-start(f32[1024,32]{0,1:T(8,128)} %copy-done.27) | copy-start | bytes 393220
  1362.3 28.9 %copy-start.30 = (f32[1024,32]{0,1:T(8,128)S(1)}, f32[1024,32]{0,1:T(8,128)}, u32[]{:S(2)}) copy-start(f32[1024,32]{0,1:T(8,128)} %copy-done.29) | copy-start | bytes 393220
  1393.1 258.7 %all-reduce.16.cloned.1.call-start = ((), (), s32[]{:S(2)}) async-start(), calls=%async_computation.23 | async-start | bytes 1744896 | tf_op jit(solution)/shard_map/psum | solution.py:259
  (91 other events, 488.3 us)
Sparse Core Ops, SparseCore 0:
  78.1 17.0 all-gather.5
  112.6 17.0 all-gather.7
  131.9 51.6 all-gather.11
  185.6 45.4 all-gather.9
  233.2 46.5 all-gather.13
  945.6 36.0 reduce-scatter.29
  985.6 63.4 reduce-scatter.33
  1052.9 62.2 reduce-scatter.31
  1194.9 35.6 reduce-scatter.27
  1234.1 84.3 reduce-scatter.25
  1322.5 78.8 reduce-scatter.21
  1405.4 78.7 reduce-scatter.23
  1487.8 61.6 reduce-scatter.19
  1552.6 61.1 reduce-scatter.17
  1617.2 34.5 all-reduce.15
where the time goes:
time: 1690 us; the launch traced here: 1670 us
  local copies, waits for them, and re-layouts  854 us (51%)
  matrix products  260 us (15%)
  waiting for transfers between devices  210 us (12%)
  blocking collectives  184 us (11%)
  other arithmetic  140 us (8%)
    unnamed x136, local copies, waits for them, and re-layouts  641 us
    dot_general x42, matrix products, product(): jnp.einsum(pattern, left_side, right_side, preferred_element_type=jnp.flo...  237 us
    dynamic_update_slice x8, local copies, waits for them, and re-layouts, body(): lax.map(back_sequence, (query_blocks, grad_blocks, log_total, keys_seqs,...  117 us
    reduce_scatter x1, waiting for transfers between devices, body(): lax.psum_scatter(grad_key, 'fsdp', scatter_dimension=0, tiled=True)  63.4 us
    reduce_scatter x1, waiting for transfers between devices, body(): lax.psum_scatter(grad_up, 'fsdp', scatter_dimension=0, tiled=True)  62.8 us
    reduce_scatter x1, waiting for transfers between devices, body(): lax.psum_scatter(grad_value, 'fsdp', scatter_dimension=0, tiled=True)  59 us
    convert_element_type x4, other arithmetic, backward_block(): (probability * (grad_probability - inner_sum)).astype(jnp.bfloat16)  55.3 us
    reduce_sum x4, other arithmetic, forward_block(): totals = jnp.sum(raised, axis=-1, keepdims=True)  44.3 us
  transfers between devices with their start and end apart: 15, of which 4 were waited for; matrix products, arithmetic and copies ran while one was open for 38% of the time, Pallas kernels for 0%

commit v1 on v0

v1 whole, which is shorter than its diff:
```python
import functools

import jax
import jax.numpy as jnp
from jax import lax
from jax.experimental import pallas as pl
from jax.experimental.pallas import tpu as pltpu
from jax.sharding import PartitionSpec as P

Q_HEADS = 9
KV_HEADS = 3
HEAD = 64
GROUP = Q_HEADS // KV_HEADS
PAD = 128

epsilon = 1e-05
rope_base = 100000.0


def rms_norm(values, gain_vector):
    scaling = lax.rsqrt(jnp.mean(values * values, axis=-1, keepdims=True) + epsilon)
    return values * scaling * gain_vector


def rope_tables(positions):
    half_size = HEAD // 2
    frequency = rope_base ** (-2.0 * jnp.arange(half_size, dtype=jnp.float32) / HEAD)
    angles = frequency[:, None] * positions.astype(jnp.float32)[None, :]
    return jnp.cos(angles), jnp.sin(angles)


def rotate(features, cosine, sine_part):
    count = features.shape[1]
    pairs = features.reshape(-1, 2, HEAD // 2, count)
    first, second = pairs[:, 0], pairs[:, 1]
    turned = jnp.stack(
        [first * cosine - second * sine_part, second * cosine + first * sine_part], axis=1
    )
    return turned.reshape(features.shape)


def product(left_side, right_side, pattern):
    return jnp.einsum(pattern, left_side, right_side, preferred_element_type=jnp.float32)


def swish_gate(gate_in, upper_in):
    return jax.nn.silu(gate_in) * upper_in


def mm(left_side, right_side):
    return jnp.dot(left_side, right_side, preferred_element_type=jnp.float32)


def mm_nt(left_side, right_side):
    return lax.dot_general(
        left_side, right_side, (((1,), (1,)), ((), ())), preferred_element_type=jnp.float32
    )


def causal(span):
    shape = (span, GROUP * span)
    key_at = lax.broadcasted_iota(jnp.int32, shape, 0)
    query_at = lax.rem(lax.broadcasted_iota(jnp.int32, shape, 1), span)
    return key_at <= query_at


def heads_side_by_side(ref, part, span):
    columns = slice(part * span, (part + 1) * span)
    return jnp.concatenate(
        [ref[g * HEAD : (g + 1) * HEAD, columns] for g in range(GROUP)], axis=1
    )


def forward_kernel(span, holder_ref, place_ref, q_ref, kv_ref, o_ref, lse_ref, keys, values):
    spans = keys.shape[0]
    for c in range(spans // 2):
        for half in range(2):
            columns = slice(half * span, (half + 1) * span)
            keys[2 * c + half] = kv_ref[c, 0, :, columns].T
            values[2 * c + half] = kv_ref[c, 1, :, columns]
    for part in range(2):
        query = heads_side_by_side(q_ref, part, span)
        place = place_ref[part]
        own = holder_ref[place]
        scores = jnp.where(causal(span), mm(keys[own], query), -1e30)
        top = jnp.max(scores, axis=0, keepdims=True)
        raised = jnp.exp(scores - top)
        total = jnp.sum(raised, axis=0, keepdims=True)
        mixed = mm(values[own], raised.astype(jnp.bfloat16))

        def earlier(j, carry, query=query):
            top, total, mixed = carry
            held = holder_ref[j]
            scores = mm(keys[held], query)
            new_top = jnp.maximum(top, jnp.max(scores, axis=0, keepdims=True))
            shrink = jnp.exp(top - new_top)
            raised = jnp.exp(scores - new_top)
            total = total * shrink + jnp.sum(raised, axis=0, keepdims=True)
            mixed = mixed * shrink + mm(values[held], raised.astype(jnp.bfloat16))
            return new_top, total, mixed

        top, total, mixed = lax.fori_loop(0, place, earlier, (top, total, mixed))
        mixed = mixed / total
        lse = top + jnp.log(total)
        for g in range(GROUP):
            source = slice(g * span, (g + 1) * span)
            columns = slice(part * span, (part + 1) * span)
            o_ref[g * HEAD : (g + 1) * HEAD, columns] = mixed[:, source].astype(jnp.bfloat16)
            lse_ref[0, g : g + 1, columns] = lse[:, source]


def backward_kernel(
    span, holder_ref, place_ref, q_ref, do_ref, o_ref, lse_ref, kv_ref,
    dq_ref, dkv_ref, keys, keys_t, values, key_sum, value_sum, query_sum,
):
    spans = keys.shape[0]
    for c in range(spans // 2):
        for half in range(2):
            columns = slice(half * span, (half + 1) * span)
            keys[2 * c + half] = kv_ref[c, 0, :, columns].T
            keys_t[2 * c + half] = kv_ref[c, 0, :, columns]
            values[2 * c + half] = kv_ref[c, 1, :, columns].T
    key_sum[...] = jnp.zeros_like(key_sum)
    value_sum[...] = jnp.zeros_like(value_sum)
    for part in range(2):
        query = heads_side_by_side(q_ref, part, span)
        upstream = heads_side_by_side(do_ref, part, span)
        mixed = heads_side_by_side(o_ref, part, span)
        columns = slice(part * span, (part + 1) * span)
        lse = jnp.concatenate([lse_ref[0, g : g + 1, columns] for g in range(GROUP)], axis=1)
        delta = jnp.sum(
            upstream.astype(jnp.float32) * mixed.astype(jnp.float32), axis=0, keepdims=True
        )
        place = place_ref[part]

        def block(held, masked, query=query, upstream=upstream, lse=lse, delta=delta):
            scores = mm(keys[held], query)
            if masked:
                scores = jnp.where(causal(span), scores, -1e30)
            probability = jnp.exp(scores - lse)
            grad_probability = mm(values[held], upstream)
            grad_scores = (probability * (grad_probability - delta)).astype(jnp.bfloat16)
            value_sum[held] += mm_nt(probability.astype(jnp.bfloat16), upstream)
            key_sum[held] += mm_nt(grad_scores, query)
            return mm(keys_t[held], grad_scores)

        query_sum[...] = block(holder_ref[place], True)

        def earlier(j, carry, block=block):
            query_sum[...] += block(holder_ref[j], False)
            return carry

        lax.fori_loop(0, place, earlier, 0)
        for g in range(GROUP):
            dq_ref[g * HEAD : (g + 1) * HEAD, columns] = query_sum[:, g * span : (g + 1) * span]
    for c in range(spans // 2):
        for half in range(2):
            columns = slice(half * span, (half + 1) * span)
            dkv_ref[c, 0, :, columns] = key_sum[2 * c + half].T.astype(jnp.bfloat16)
            dkv_ref[c, 1, :, columns] = value_sum[2 * c + half].T.astype(jnp.bfloat16)


def attention_specs(local_rows, context_size):
    wide = pl.BlockSpec((GROUP * HEAD, local_rows), lambda b, k, *_: (k, b))
    total = pl.BlockSpec((1, GROUP, local_rows), lambda b, k, *_: (k, 0, b))
    shared = pl.BlockSpec((context_size, 2, HEAD, local_rows), lambda b, k, *_: (0, 0, k, b))
    return wide, total, shared


def attend(holder, places, queries, kv_every, local_rows):
    width, tokens = queries.shape
    context_size = kv_every.shape[0]
    span, spans = local_rows // 2, 2 * context_size
    wide, total, shared = attention_specs(local_rows, context_size)
    work = width * tokens * spans * span
    return pl.pallas_call(
        functools.partial(forward_kernel, span),
        out_shape=(
            jax.ShapeDtypeStruct((width, tokens), jnp.bfloat16),
            jax.ShapeDtypeStruct((KV_HEADS, GROUP, tokens), jnp.float32),
        ),
        grid_spec=pltpu.PrefetchScalarGridSpec(
            num_scalar_prefetch=2,
            grid=(tokens // local_rows, KV_HEADS),
            in_specs=[wide, shared],
            out_specs=(wide, total),
            scratch_shapes=[
                pltpu.VMEM((spans, span, HEAD), jnp.bfloat16),
                pltpu.VMEM((spans, HEAD, span), jnp.bfloat16),
            ],
        ),
        compiler_params=pltpu.CompilerParams(vmem_limit_bytes=32 * 1024 * 1024),
        cost_estimate=pl.CostEstimate(
            flops=16 * work, bytes_accessed=8 * width * tokens, transcendentals=work // HEAD
        ),
        name="attend",
    )(holder, places, queries, kv_every)


def attend_back(holder, places, queries, upstream, mixed, lse, kv_every, local_rows):
    width, tokens = queries.shape
    context_size = kv_every.shape[0]
    span, spans = local_rows // 2, 2 * context_size
    wide, total, shared = attention_specs(local_rows, context_size)
    work = width * tokens * spans * span
    return pl.pallas_call(
        functools.partial(backward_kernel, span),
        out_shape=(
            jax.ShapeDtypeStruct((width, tokens), jnp.float32),
            jax.ShapeDtypeStruct(kv_every.shape, jnp.bfloat16),
        ),
        grid_spec=pltpu.PrefetchScalarGridSpec(
            num_scalar_prefetch=2,
            grid=(tokens // local_rows, KV_HEADS),
            in_specs=[wide, wide, wide, total, shared],
            out_specs=(wide, shared),
            scratch_shapes=[
                pltpu.VMEM((spans, span, HEAD), jnp.bfloat16),
                pltpu.VMEM((spans, HEAD, span), jnp.bfloat16),
                pltpu.VMEM((spans, span, HEAD), jnp.bfloat16),
                pltpu.VMEM((spans, span, HEAD), jnp.float32),
                pltpu.VMEM((spans, span, HEAD), jnp.float32),
                pltpu.VMEM((HEAD, GROUP * span), jnp.float32),
            ],
        ),
        compiler_params=pltpu.CompilerParams(vmem_limit_bytes=32 * 1024 * 1024),
        cost_estimate=pl.CostEstimate(
            flops=40 * work, bytes_accessed=16 * width * tokens, transcendentals=work // HEAD
        ),
        name="attend_back",
    )(holder, places, queries, upstream, mixed, lse, kv_every)


def body(
    tokens,
    cotangent,
    span_order,
    norm_one,
    w_query,
    w_key,
    w_value,
    w_out,
    norm_two,
    w_gate,
    w_up,
    w_down,
):
    sequences, local_rows, model_width = tokens.shape
    span_size = local_rows // 2
    key_width = KV_HEADS * HEAD
    query_width = Q_HEADS * HEAD
    qkv_width = query_width + 2 * key_width
    attn_width = qkv_width + model_width
    token_count = sequences * local_rows
    inner_width = w_gate.shape[1]
    own_spans = lax.dynamic_slice_in_dim(span_order, lax.axis_index("ctx") * 2, 2)
    holder = jnp.argsort(span_order).astype(jnp.int32)
    own_places = (
        own_spans[:, None] * span_size + jnp.arange(span_size, dtype=jnp.int32)[None, :]
    ).reshape(local_rows)
    cosine, sine_part = rope_tables(jnp.tile(own_places, sequences))

    gains = jnp.stack([norm_one, norm_two], axis=1)
    attn_shard = jnp.concatenate(
        [w_query, w_key, w_value, w_out, jnp.pad(gains, ((0, 0), (0, PAD - 2)))], axis=1
    )
    attn_every = lax.all_gather(attn_shard, "fsdp", axis=0, tiled=True)
    gate_up = lax.all_gather(
        jnp.concatenate([w_gate, w_up], axis=1), "fsdp", axis=0, tiled=True
    )
    down_matrix = lax.all_gather(w_down, "fsdp", axis=0, tiled=True)
    qkv_matrix = attn_every[:, :qkv_width]
    out_matrix = attn_every[:, qkv_width:attn_width]
    gain_one = attn_every[:, attn_width].astype(jnp.float32)
    gain_two = attn_every[:, attn_width + 1].astype(jnp.float32)

    hidden_in = tokens.reshape(token_count, model_width).astype(jnp.float32)
    normed = rms_norm(hidden_in, gain_one).astype(jnp.bfloat16)
    kv_pre = product(qkv_matrix[:, query_width:], normed, "dh,nd->hn")
    keys_own = rotate(kv_pre[:key_width], cosine, sine_part).astype(jnp.bfloat16)
    kv_own = jnp.stack([keys_own, kv_pre[key_width:].astype(jnp.bfloat16)], axis=0)
    kv_every = lax.all_gather(kv_own, "ctx", axis=0, tiled=False)
    query_pre = product(qkv_matrix[:, :query_width], normed, "dh,nd->hn")
    queries = (rotate(query_pre, cosine, sine_part) * 0.125).astype(jnp.bfloat16)

    attended, lse = attend(holder, own_spans, queries, kv_every, local_rows)
    middle = hidden_in + product(attended, out_matrix, "hn,hd->nd")

    normed_two = rms_norm(middle, gain_two).astype(jnp.bfloat16)
    gate_pre = mm(normed_two, gate_up[:, :inner_width])
    up_pre = mm(normed_two, gate_up[:, inner_width:])
    inner_act = swish_gate(gate_pre, up_pre).astype(jnp.bfloat16)
    output = middle + mm(inner_act, down_matrix)

    upstream_low = cotangent.reshape(token_count, model_width)
    upstream = upstream_low.astype(jnp.float32)
    grad_inner = product(upstream_low, down_matrix, "nd,fd->nf")
    _, inner_pull = jax.vjp(swish_gate, gate_pre, up_pre)
    grad_gate_pre, grad_up_pre = inner_pull(grad_inner)
    grad_gate_up_pre = jnp.concatenate(
        [grad_gate_pre.astype(jnp.bfloat16), grad_up_pre.astype(jnp.bfloat16)], axis=1
    )
    grad_normed_two = product(grad_gate_up_pre, gate_up, "nf,df->nd")
    grad_down = product(inner_act, upstream_low, "nf,nd->fd").astype(jnp.bfloat16)
    grad_gate_up = product(normed_two, grad_gate_up_pre, "nd,nf->df").astype(jnp.bfloat16)
    down_part = lax.psum_scatter(grad_down, "fsdp", scatter_dimension=0, tiled=True)
    gate_up_part = lax.psum_scatter(grad_gate_up, "fsdp", scatter_dimension=0, tiled=True)

    _, second_pull = jax.vjp(rms_norm, middle, gain_two)
    grad_middle_norm, grad_gain_two = second_pull(grad_normed_two)
    grad_middle = upstream + grad_middle_norm
    middle_low = grad_middle.astype(jnp.bfloat16)
    grad_attended = product(out_matrix, middle_low, "hd,nd->hn").astype(jnp.bfloat16)

    query_grads, kv_grads = attend_back(
        holder, own_spans, queries, grad_attended, attended, lse, kv_every, local_rows
    )
    kv_mine = lax.psum_scatter(kv_grads, "ctx", scatter_dimension=0, tiled=False)
    grad_out = product(attended, middle_low, "hn,nd->hd")
    query_low = (rotate(query_grads, cosine, -sine_part) * 0.125).astype(jnp.bfloat16)
    key_low = rotate(kv_mine[0].astype(jnp.float32), cosine, -sine_part).astype(jnp.bfloat16)
    qkv_low = jnp.concatenate([query_low, key_low, kv_mine[1]], axis=0)
    grad_qkv = product(normed, qkv_low, "nd,hn->dh")
    grad_normed = product(qkv_low, qkv_matrix, "hn,dh->nd")
    _, first_pull = jax.vjp(rms_norm, hidden_in, gain_one)
    grad_hidden_norm, grad_gain_one = first_pull(grad_normed)
    grad_input = grad_middle + grad_hidden_norm

    grad_gains = jnp.pad(
        jnp.stack([grad_gain_one, grad_gain_two], axis=1), ((0, 0), (0, PAD - 2))
    )
    attn_grads = jnp.concatenate([grad_qkv, grad_out, grad_gains], axis=1).astype(jnp.bfloat16)
    attn_part = lax.psum_scatter(attn_grads, "fsdp", scatter_dimension=0, tiled=True)
    down_sum = lax.psum(down_part, "ctx").astype(jnp.float32)
    gate_up_sum = lax.psum(gate_up_part, "ctx").astype(jnp.float32)
    attn_sum = lax.psum(attn_part, "ctx").astype(jnp.float32)
    key_start = query_width
    value_start = query_width + key_width
    return (
        output.astype(jnp.bfloat16).reshape(tokens.shape),
        grad_input.reshape(tokens.shape),
        attn_sum[:, attn_width],
        attn_sum[:, :key_start],
        attn_sum[:, key_start:value_start],
        attn_sum[:, value_start:qkv_width],
        attn_sum[:, qkv_width:attn_width],
        attn_sum[:, attn_width + 1],
        gate_up_sum[:, :inner_width],
        gate_up_sum[:, inner_width:],
        down_sum,
    )


def solution(mesh):
    in_specs = (
        P("fsdp", "ctx", None),
        P("fsdp", "ctx", None),
        P(),
        P("fsdp"),
        P("fsdp", None),
        P("fsdp", None),
        P("fsdp", None),
        P("fsdp", None),
        P("fsdp"),
        P("fsdp", None),
        P("fsdp", None),
        P("fsdp", None),
    )
    out_specs = (
        P("fsdp", "ctx", None),
        P("fsdp", "ctx", None),
        P("fsdp"),
        P("fsdp", None),
        P("fsdp", None),
        P("fsdp", None),
        P("fsdp", None),
        P("fsdp"),
        P("fsdp", None),
        P("fsdp", None),
        P("fsdp", None),
    )
    return jax.shard_map(body, mesh=mesh, in_specs=in_specs, out_specs=out_specs, check_vma=False)
```

time: 1690 us -> 593 us (0.35); the launches traced: 1670 us -> 587 us
  local copies, waits for them, and re-layouts: 854 us -> 36.7 us
  matrix products: 260 us -> 67.7 us
  blocking collectives: 184 us -> 0 us
  waiting for transfers between devices: 210 us -> 369 us
  other arithmetic: 140 us -> 21.8 us
  Pallas kernels: 0 us -> 76.8 us
    unnamed x136 -> x93, local copies, waits for them, and re-layouts: 641 us -> 7.69 us
    dot_general x42 -> x11, matrix products: 237 us -> 48.7 us  [product(): jnp.einsum(pattern, left_side, right_side, preferred_element_type=jnp.flo...]
    all_gather x4 -> x0, blocking collectives: 130 us -> none  [the longest x1 35.4 us: body(): lax.all_gather(w_out, 'fsdp', axis=0, tiled=True)]
    dynamic_update_slice x14 -> x0, local copies, waits for them, and re-layouts: 124 us -> none  [the longest x8 117 us: body(): lax.map(back_sequence, (query_blocks, grad_blocks, log_total, keys_seqs,...]
    all_gather x5 -> x4, waiting for transfers between devices: 0.03 us -> 119 us  [the longest x1 44.2 us: body(): attn_every = lax.all_gather(attn_shard, 'fsdp', axis=0, tiled=True)]
    reduce_scatter x4 -> x2, waiting for transfers between devices: 185 us -> 102 us  [the longest x1 81.7 us: body(): lax.psum_scatter(grad_gate_up, 'fsdp', scatter_dimension=0, tiled=True)]
    pallas_call x0 -> x2, Pallas kernels: none -> 76.8 us  [the longest x1 43 us: attend_back(): pl.pallas_call(functools.partial(backward_kernel, span), out_shape=(jax.S...]
    convert_element_type x28 -> x8, other arithmetic: 79.4 us -> 6.53 us  [the longest x1 1.83 us: body(): gain_two = attn_every[:, attn_width + 1].astype(jnp.float32)]
  transfers between devices with their start and end apart: 15 -> 9, of which waited for: 4 -> 9; matrix products, arithmetic and copies ran while one was open for 38% -> 15% of each run, Pallas kernels for 0% -> 6%
where the time goes in v1:
time: 593 us; the launch traced here: 587 us
  waiting for transfers between devices  369 us (62%)
  Pallas kernels  76.8 us (13%)
  matrix products  67.7 us (11%)
  local copies, waits for them, and re-layouts  36.7 us (6%)
  other arithmetic  21.8 us (4%)
  between operations  14.9 us (3%)
    reduce_scatter x1, waiting for transfers between devices, body(): lax.psum_scatter(grad_gate_up, 'fsdp', scatter_dimension=0, tiled=True)  81.7 us
    unnamed x10, waiting for transfers between devices  70 us
    dot_general x11, matrix products, product(): jnp.einsum(pattern, left_side, right_side, preferred_element_type=jnp.flo...  48.7 us
    reduce_scatter x1, waiting for transfers between devices, body(): lax.psum_scatter(grad_down, 'fsdp', scatter_dimension=0, tiled=True)  45.8 us
    all_gather x1, waiting for transfers between devices, body(): attn_every = lax.all_gather(attn_shard, 'fsdp', axis=0, tiled=True)  44.2 us
    pallas_call x1, Pallas kernels, attend_back(): pl.pallas_call(functools.partial(backward_kernel, span), out_shape=(jax.S...  43 us
    all_gather x1, waiting for transfers between devices, body(): down_matrix = lax.all_gather(w_down, 'fsdp', axis=0, tiled=True)  37.1 us
    pallas_call x1, Pallas kernels, attend(): pl.pallas_call(functools.partial(forward_kernel, span), out_shape=(jax.Sh...  33.8 us
  transfers between devices with their start and end apart: 9, of which 9 were waited for; matrix products, arithmetic and copies ran while one was open for 15% of the time, Pallas kernels for 6%

profile of v1, /device:TPU:0, one launch (start us, length us, event | category | flops | bytes accessed | tf_op | source)
XLA Modules:
  0.0 587.5 jit_solution(3839509164838118493)
XLA Ops:
  16.4 44.2 %all-gather.6.cloned.1.call-done = bf16[576,1664]{1,0:T(8,128)(2,1)} async-done(((bf16[72,1664]{1,0:T(8,128)(2,1)}), bf16[576,1664]{1,0:T(8,128)(2,1)}) %all-gather.6.cloned.1.call-update) | async-done | bytes 1916944 | tf_op jit(solution)/shard_map/all_gather | solution.py:267
  62.4 2.2 fusion.24
  65.9 1.8 pad_maximum_fusion.7
  70.0 2.6 copy.51
  72.6 37.1 %all-gather.10.cloned.1.call-done = bf16[1536,576]{1,0:T(8,128)(2,1)} async-done(((bf16[192,576]{1,0:T(8,128)(2,1)}), bf16[1536,576]{1,0:T(8,128)(2,1)}) %all-gather.10.cloned.1.call-update) | async-done | bytes 1769488 | tf_op jit(solution)/shard_map/all_gather | solution.py:271
  109.7 7.2 %fusion.39 = f32[1024,1536]{1,0:T(8,128)} fusion(bf16[1024,576]{0,1:T(8,128)(2,1)} %bitcast.70, bf16[1536,576]{1,0:T(8,128)(2,1)} %all-gather.10.cloned.1.call-done), kind=kOutput, calls=%fused_computation.99 | convolution fusion | flops 1811939328 | bytes 9240576 | tf_op jit(solution)/shard_map/nd,fd->nf/dot_general | solution.py:43
  116.9 2.1 slice_bitcast_fusion
  119.0 2.4 copy.40
  125.4 2.6 fusion.18
  128.9 10.5 %all-gather.12.cloned.1.call-done = bf16[8,192,1024]{2,1,0:T(8,128)(2,1)} async-done(((bf16[2,192,1024]{2,1,0:T(8,128)(2,1)}), bf16[8,192,1024]{2,1,0:T(8,128)(2,1)}) %all-gather.12.cloned.1.call-update) | async-done | bytes 3145744 | tf_op jit(solution)/shard_map/all_gather | solution.py:282
  139.4 1.9 copy-done.3
  141.3 33.8 %attend.1 = (bf16[576,1024]{1,0:T(8,128)(2,1)S(1)}, f32[3,3,1024]{2,1,0:T(4,128)S(1)}) custom-call(s32[8]{0:T(128)S(1)} %get-tuple-element.16.holder_ref, s32[2]{0:T(128)S(1)} %get-tuple-element.66.place_ref, bf16[576,1024]{1,0:T(8,128)(2,1)S(1)} %bitcast.60, bf16[4,2,192,1024]{3,2,1,0:T(8,128)(2,1)S(1)} %bitcast.62), custom_call_target="tpu_custom_call" | custom-call | flops 19327352832 | bytes 4718592 | tf_op jit(solution)/shard_map/attend/pallas_call | solution.py:176
  175.2 3.0 multiply_reduce_fusion.4
  180.0 27.3 %all-gather.8.cloned.1.call-done = bf16[576,3072]{1,0:T(8,128)(2,1)} async-done(((bf16[72,3072]{1,0:T(8,128)(2,1)}), bf16[576,3072]{1,0:T(8,128)(2,1)}) %all-gather.8.cloned.1.call-update) | async-done | bytes 3538960 | tf_op jit(solution)/shard_map/all_gather | solution.py:268
  207.3 4.3 fusion.12
  211.7 9.3 %fusion.2 = (bf16[1024,1536]{1,0:T(8,128)(2,1)S(1)}, bf16[1024,1536]{1,0:T(8,128)(2,1)S(1)}, bf16[1024,1536]{1,0:T(8,128)(2,1)}) fusion(f32[1024,1536]{1,0:T(8,128)} %fusion.39, f32[1024,1536]{1,0:T(8,128)S(1)} %fusion.12, bf16[1024,576]{0,1:T(8,128)(2,1)} %copy-done.22, bf16[576,3072]{1,0:T(8,128)(2,1)S(1)} %copy-done.41), kind=kOutput, calls=%fused_computation.3 | convolution fusion | flops 1837105152 | bytes 24969216 | tf_op jit(solution)/shard_map/dot_general | solution.py:51
  221.1 4.7 multiply_reduce_fusion
  226.5 3.1 convolution_convert_fusion.3.do_ref
  229.9 43.0 %attend_back.1 = (f32[576,1024]{1,0:T(8,128)S(1)}, bf16[4,2,192,1024]{3,2,1,0:T(8,128)(2,1)}) custom-call(s32[8]{0:T(128)S(1)} %get-tuple-element.16.holder_ref, s32[2]{0:T(128)S(1)} %get-tuple-element.66.place_ref, bf16[576,1024]{1,0:T(8,128)(2,1)S(1)} %bitcast.61, bf16[576,1024]{1,0:T(8,128)(2,1)S(1)} %convolution_convert_fusion.3.do_ref, ...), custom_call_target="tpu_custom_call" | custom-call | flops 48318382080 | bytes 9437184 | tf_op jit(solution)/shard_map/attend_back/pallas_call | solution.py:206
  274.1 5.8 convolution_convert_fusion.1
  280.3 9.3 %convolution_convert_fusion = bf16[576,3072]{1,0:T(8,128)(2,1)} fusion(bf16[1024,576]{0,1:T(8,128)(2,1)} %copy-done.22, bf16[1024,1536]{1,0:T(8,128)(2,1)} %copy-done.43, bf16[1024,1536]{1,0:T(8,128)(2,1)} %copy-done.42), kind=kOutput, calls=%fused_computation.9 | convolution fusion | flops 3638231040 | bytes 11010048 | tf_op jit(solution)/shard_map/nd,nf->df/dot_general | solution.py:43
  293.4 2.0 convolution_convert_fusion.4
  295.4 19.8 %reduce-scatter.7.cloned.1.call-done = bf16[1,2,192,1024]{3,2,1,0:T(8,128)(2,1)} async-done(((bf16[4,2,192,1024]{3,2,1,0:T(8,128)(2,1)}), bf16[1,2,192,1024]{3,2,1,0:T(8,128)(2,1)}) %reduce-scatter.7.cloned.1.call-update) | async-done | bytes 786448 | tf_op jit(solution)/shard_map/reduce_scatter | solution.py:318
  317.0 5.0 multiply_reduce_fusion.1
  325.7 3.6 convolution_convert_fusion.2
  329.3 4.1 concatenate.20
  333.4 5.3 add_convert_fusion
  339.9 45.8 %reduce-scatter.11.cloned.1.call-done = bf16[192,576]{1,0:T(8,128)(2,1)} async-done(((bf16[1536,576]{1,0:T(8,128)(2,1)}), bf16[192,576]{1,0:T(8,128)(2,1)}) %reduce-scatter.11.cloned.1.call-update) | async-done | bytes 221200 | tf_op jit(solution)/shard_map/reduce_scatter | solution.py:306
  385.7 81.7 %reduce-scatter.9.cloned.1.call-done = bf16[72,3072]{1,0:T(8,128)(2,1)} async-done(((bf16[576,3072]{1,0:T(8,128)(2,1)}), bf16[72,3072]{1,0:T(8,128)(2,1)}) %reduce-scatter.9.cloned.1.call-update) | async-done | bytes 442384 | tf_op jit(solution)/shard_map/reduce_scatter | solution.py:307
  467.4 69.2 %reduce-scatter.13.cloned.1.call-done = bf16[72,1664]{1,0:T(8,128)(2,1)} async-done(((bf16[576,1664]{1,0:T(8,128)(2,1)}), bf16[72,1664]{1,0:T(8,128)(2,1)}) %reduce-scatter.13.cloned.1.call-update) | async-done | bytes 239632
  536.6 2.9 fusion.6
  541.2 32.5 %all-reduce.6.cloned.1.call-done = (bf16[72,3072]{1,0:T(8,128)(2,1)}, bf16[72,1664]{1,0:T(8,128)(2,1)}, bf16[192,576]{1,0:T(8,128)(2,1)}) async-done(((bf16[72,3072]{1,0:T(8,128)(2,1)}, bf16[72,1664]{1,0:T(8,128)(2,1)}, bf16[192,576]{1,0:T(8,128)(2,1)}), (bf16[72,3072]{1,0:T(8,128)(2,1)}, bf16[72,1664]{1,0:T(8,128)(2,1)}, bf16[192,576]{1,0:T(8,128)(2,1)})) %all-reduce.6.cloned.1.call-update) | async-done | bytes 903184 | tf_op jit(solution)/shard_map/psum | solution.py:335
  (159 shorter events, 42.1 us)
Async XLA Ops:
  7.2 7.1 %copy-start.11 = (bf16[2,512,576]{1,2,0:T(8,128)(2,1)S(1)}, bf16[2,512,576]{1,2,0:T(8,128)(2,1)}, u32[]{:S(2)}) copy-start(bf16[2,512,576]{1,2,0:T(8,128)(2,1)} %param.12) | copy-start | bytes 3538948
  7.2 53.4 %all-gather.6.cloned.1.call-start = ((), (), s32[]{:S(2)}) async-start(), calls=%async_computation.4 | async-start | bytes 2156544 | tf_op jit(solution)/shard_map/all_gather | solution.py:267
  10.0 99.7 %all-gather.10.cloned.1.call-start = ((), (), s32[]{:S(2)}) async-start(), calls=%async_computation.6 | async-start | bytes 2211840 | tf_op jit(solution)/shard_map/all_gather | solution.py:271
  10.7 128.7 %all-gather.12.cloned.1.call-start = ((), (), s32[]{:S(2)}) async-start(), calls=%async_computation.10 | async-start | bytes 3932160 | tf_op jit(solution)/shard_map/all_gather | solution.py:282
  14.8 160.4 %copy-start.7 = (f32[2,72,8,512]{3,2,0,1:T(8,128)}, f32[2,72,8,512]{3,2,0,1:T(8,128)S(1)}, u32[]{:S(2)}) copy-start(f32[2,72,8,512]{3,2,0,1:T(8,128)S(1)} %copy.50) | copy-start | bytes 7077892
  65.9 141.4 %all-gather.8.cloned.1.call-start = ((), (), s32[]{:S(2)}) async-start(), calls=%async_computation.5 | async-start | bytes 3981312 | tf_op jit(solution)/shard_map/all_gather | solution.py:268
  67.8 247.4 %reduce-scatter.7.cloned.1.call-start = ((), (), s32[]{:S(2)}) async-start(), calls=%async_computation.7 | async-start | bytes 3932160 | tf_op jit(solution)/shard_map/reduce_scatter | solution.py:318
  175.2 4.5 copy-start.31
  178.3 29.0 %copy-start.33 = (f32[1024]{0:T(1024)}, f32[1024]{0:T(1024)S(1)}, u32[]{:S(2)}) copy-start(f32[1024]{0:T(1024)S(1)} %fusion.28) | copy-start | bytes 12292
  179.9 27.4 %copy-start.22 = (bf16[1024,576]{0,1:T(8,128)(2,1)}, bf16[1024,576]{0,1:T(8,128)(2,1)S(1)}, u32[]{:S(2)}) copy-start(bf16[1024,576]{0,1:T(8,128)(2,1)S(1)} %multiply_convert_fusion.2) | copy-start | bytes 3538948
  207.3 4.3 copy-start.41
  211.7 9.4 %copy-start.10 = (f32[1024,576]{0,1:T(8,128)S(1)}, f32[1024,576]{0,1:T(8,128)}, u32[]{:S(2)}) copy-start(f32[1024,576]{0,1:T(8,128)} %copy-done.9) | copy-start | bytes 7077892
  211.7 9.4 %copy-start.32 = (f32[576]{0:T(1024)S(1)}, f32[576]{0:T(1024)}, u32[]{:S(2)}) copy-start(f32[576]{0:T(1024)} %get-tuple-element.58) | copy-start | bytes 6916
  211.7 9.4 %copy-start.34 = (f32[1024]{0:T(1024)S(1)}, f32[1024]{0:T(1024)}, u32[]{:S(2)}) copy-start(f32[1024]{0:T(1024)} %copy-done.33) | copy-start | bytes 12292
  221.0 4.8 copy-start.42
  221.1 4.8 copy-start.43
  221.1 4.7 copy-start.38
  221.1 4.7 copy-start.14
  226.5 3.4 copy-start.4
  226.5 3.4 copy-start.6
  272.9 112.8 %reduce-scatter.11.cloned.1.call-start = ((), (), s32[]{:S(2)}) async-start(), calls=%async_computation.9 | async-start | bytes 2211840 | tf_op jit(solution)/shard_map/reduce_scatter | solution.py:306
  280.0 187.4 %reduce-scatter.9.cloned.1.call-start = ((), (), s32[]{:S(2)}) async-start(), calls=%async_computation.8 | async-start | bytes 3981312 | tf_op jit(solution)/shard_map/reduce_scatter | solution.py:307
  289.6 247.0 %reduce-scatter.13.cloned.1.call-start = ((), (), s32[]{:S(2)}) async-start(), calls=%async_computation.11 | async-start | bytes 2156544
  295.4 21.2 %copy-start.19 = (f32[32,1024]{1,0:T(8,128)S(1)}, f32[32,1024]{1,0:T(8,128)}, u32[]{:S(2)}) copy-start(f32[32,1024]{1,0:T(8,128)} %get-tuple-element.88) | copy-start | bytes 393220
  295.4 21.2 %copy-start.25 = (f32[32,1024]{1,0:T(8,128)S(1)}, f32[32,1024]{1,0:T(8,128)}, u32[]{:S(2)}) copy-start(f32[32,1024]{1,0:T(8,128)} %get-tuple-element.86) | copy-start | bytes 393220
  295.4 21.4 %copy-start.8 = (f32[2,72,8,512]{3,2,0,1:T(8,128)S(1)}, f32[2,72,8,512]{3,2,0,1:T(8,128)}, u32[]{:S(2)}) copy-start(f32[2,72,8,512]{3,2,0,1:T(8,128)} %copy-done.7) | copy-start | bytes 7077892
  316.5 5.5 copy-start.29
  316.8 5.2 copy-start.28
  317.0 8.7 %copy-start.23 = (bf16[9,2,32,1024]{3,2,1,0:T(8,128)(2,1)S(1)}, bf16[9,2,32,1024]{3,2,1,0:T(8,128)(2,1)}, u32[]{:S(2)}) copy-start(bf16[9,2,32,1024]{3,2,1,0:T(8,128)(2,1)} %fusion.11) | copy-start | bytes 3538948
  333.4 240.3 %all-reduce.6.cloned.1.call-start = ((), (), s32[]{:S(2)}) async-start(), calls=%async_computation.12 | async-start | bytes 1855488 | tf_op jit(solution)/shard_map/psum | solution.py:335
  573.7 5.0 copy-start.21
  573.7 6.0 %copy-start.30 = (bf16[192,576]{1,0:T(8,128)(2,1)S(1)}, bf16[192,576]{1,0:T(8,128)(2,1)}, u32[]{:S(2)}) copy-start(bf16[192,576]{1,0:T(8,128)(2,1)} %get-tuple-element.64) | copy-start | bytes 663556
  (21 other events, 38.4 us)
Sparse Core Ops, SparseCore 0:
  10.8 49.7 all-gather.5
  62.7 46.8 all-gather.9
  111.8 27.5 all-gather.11
  142.1 65.2 all-gather.7
  273.0 42.1 reduce-scatter.6
  318.9 66.7 reduce-scatter.10
  389.3 78.0 reduce-scatter.8
  471.0 65.6 reduce-scatter.12
  539.2 34.4 all-reduce.5

commit v2 on v1

--- a/solution.py
+++ b/solution.py
@@ -12,6 +12,7 @@
 HEAD = 64
 GROUP = Q_HEADS // KV_HEADS
 PAD = 128
+GRAD_PAD = 512
 
 epsilon = 1e-05
 rope_base = 100000.0
@@ -229,6 +230,101 @@
         ),
         name="attend_back",
     )(holder, places, queries, upstream, mixed, lse, kv_every)
+
+
+def swap(values, bit):
+    size = lax.axis_size("ctx")
+    return lax.ppermute(values, "ctx", [(i, i ^ bit) for i in range(size)])
+
+
+def halve(values, bit):
+    side = (lax.axis_index("ctx") // bit) % 2
+    away = lax.dynamic_index_in_dim(values, 1 - side, 0, keepdims=False)
+    mine = lax.dynamic_index_in_dim(values, side, 0, keepdims=False)
+    came = swap(away, bit)
+    return (mine.astype(jnp.float32) + came.astype(jnp.float32)).astype(values.dtype)
+
+
+def join(values, bit):
+    side = (lax.axis_index("ctx") // bit) % 2
+    came = swap(values, bit)
+    first = jnp.where(side == 0, values, came)
+    second = jnp.where(side == 0, came, values)
+    return jnp.stack([first, second], axis=0)
+
+
+def scatter_ctx(values):
+    pairs = values.reshape((2, 2) + values.shape[1:])
+    return halve(halve(jnp.swapaxes(pairs, 0, 1), 1), 2)
+
+
+def gather_ctx(values):
+    joined = join(join(values, 2), 1)
+    return jnp.swapaxes(joined, 0, 1).reshape((4,) + values.shape)
+
+
+def scatter_fsdp(values):
+    size = lax.axis_size("fsdp")
+    if size > 8:
+        return lax.psum_scatter(values, "fsdp", scatter_dimension=0, tiled=False)
+    me = lax.axis_index("fsdp")
+    total = lax.dynamic_index_in_dim(values, me, 0, keepdims=False).astype(jnp.float32)
+    for step in range(1, size):
+        piece = lax.dynamic_index_in_dim(values, (me + step) % size, 0, keepdims=False)
+        came = lax.ppermute(piece, "fsdp", [(i, (i + step) % size) for i in range(size)])
+        total = total + came.astype(jnp.float32)
+    return total.astype(values.dtype)
+
+
+def gather_fsdp(values):
+    size = lax.axis_size("fsdp")
+    if size > 8:
+        return lax.all_gather(values, "fsdp", axis=0, tiled=False)
+    me = lax.axis_index("fsdp")
+    every = jnp.zeros((size,) + values.shape, values.dtype)
+    every = lax.dynamic_update_index_in_dim(every, values, me, 0)
+    for step in range(1, size):
+        came = lax.ppermute(values, "fsdp", [(i, (i + step) % size) for i in range(size)])
+        every = lax.dynamic_update_index_in_dim(every, came, (me - step) % size, 0)
+    return every
+
+
+def own_quarter(values):
+    return lax.dynamic_index_in_dim(values, lax.axis_index("ctx"), 0, keepdims=False)
+
+
+def column_quarters(values):
+    rows, width = values.shape
+    return jnp.stack([values[:, q * width // 4 : (q + 1) * width // 4] for q in range(4)], axis=0)
+
+
+def gather_columns(shard):
+    quarter = gather_fsdp(own_quarter(column_quarters(shard)))
+    every = gather_ctx(quarter.reshape(-1, quarter.shape[-1]))
+    return jnp.concatenate([every[q] for q in range(4)], axis=1)
+
+
+def gather_rows(shard):
+    rows, width = shard.shape
+    quarter = gather_fsdp(own_quarter(shard.reshape(4, rows // 4, width)))
+    every = gather_ctx(quarter)
+    return jnp.swapaxes(every, 0, 1).reshape(-1, width)
+
+
+def reduce_columns(values):
+    size = lax.axis_size("fsdp")
+    quarter = scatter_ctx(column_quarters(values))
+    quarter = quarter.reshape(size, -1, quarter.shape[-1])
+    every = gather_ctx(scatter_fsdp(quarter))
+    return jnp.concatenate([every[q] for q in range(4)], axis=1).astype(jnp.float32)
+
+
+def reduce_rows(values):
+    size = lax.axis_size("fsdp")
+    width = values.shape[-1]
+    quarters = jnp.swapaxes(values.reshape(size, 4, -1, width), 0, 1)
+    every = gather_ctx(scatter_fsdp(scatter_ctx(quarters)))
+    return every.reshape(-1, width).astype(jnp.float32)
 
 
 def body(
@@ -265,10 +361,8 @@
         [w_query, w_key, w_value, w_out, jnp.pad(gains, ((0, 0), (0, PAD - 2)))], axis=1
     )
     attn_every = lax.all_gather(attn_shard, "fsdp", axis=0, tiled=True)
-    gate_up = lax.all_gather(
-        jnp.concatenate([w_gate, w_up], axis=1), "fsdp", axis=0, tiled=True
-    )
-    down_matrix = lax.all_gather(w_down, "fsdp", axis=0, tiled=True)
+    gate_up = gather_columns(jnp.concatenate([w_gate, w_up], axis=1))
+    down_matrix = gather_rows(w_down)
     qkv_matrix = attn_every[:, :qkv_width]
     out_matrix = attn_every[:, qkv_width:attn_width]
     gain_one = attn_every[:, attn_width].astype(jnp.float32)
@@ -303,8 +397,8 @@
     grad_normed_two = product(grad_gate_up_pre, gate_up, "nf,df->nd")
     grad_down = product(inner_act, upstream_low, "nf,nd->fd").astype(jnp.bfloat16)
     grad_gate_up = product(normed_two, grad_gate_up_pre, "nd,nf->df").astype(jnp.bfloat16)
-    down_part = lax.psum_scatter(grad_down, "fsdp", scatter_dimension=0, tiled=True)
-    gate_up_part = lax.psum_scatter(grad_gate_up, "fsdp", scatter_dimension=0, tiled=True)
+    down_sum = reduce_rows(grad_down)
+    gate_up_sum = reduce_columns(grad_gate_up)
 
     _, second_pull = jax.vjp(rms_norm, middle, gain_two)
     grad_middle_norm, grad_gain_two = second_pull(grad_normed_two)
@@ -315,7 +409,7 @@
     query_grads, kv_grads = attend_back(
         holder, own_spans, queries, grad_attended, attended, lse, kv_every, local_rows
     )
-    kv_mine = lax.psum_scatter(kv_grads, "ctx", scatter_dimension=0, tiled=False)
+    kv_mine = scatter_ctx(kv_grads)
     grad_out = product(attended, middle_low, "hn,nd->hd")
     query_low = (rotate(query_grads, cosine, -sine_part) * 0.125).astype(jnp.bfloat16)
     key_low = rotate(kv_mine[0].astype(jnp.float32), cosine, -sine_part).astype(jnp.bfloat16)
@@ -327,13 +421,10 @@
     grad_input = grad_middle + grad_hidden_norm
 
     grad_gains = jnp.pad(
-        jnp.stack([grad_gain_one, grad_gain_two], axis=1), ((0, 0), (0, PAD - 2))
+        jnp.stack([grad_gain_one, grad_gain_two], axis=1), ((0, 0), (0, GRAD_PAD - 2))
     )
     attn_grads = jnp.concatenate([grad_qkv, grad_out, grad_gains], axis=1).astype(jnp.bfloat16)
-    attn_part = lax.psum_scatter(attn_grads, "fsdp", scatter_dimension=0, tiled=True)
-    down_sum = lax.psum(down_part, "ctx").astype(jnp.float32)
-    gate_up_sum = lax.psum(gate_up_part, "ctx").astype(jnp.float32)
-    attn_sum = lax.psum(attn_part, "ctx").astype(jnp.float32)
+    attn_sum = reduce_columns(attn_grads)
     key_start = query_width
     value_start = query_width + key_width
     return (

time: 593 us -> 422 us (0.71); the launches traced: 587 us -> 426 us
  waiting for transfers between devices: 369 us -> 78.5 us
  starting transfers between devices: 0.62 us -> 77.2 us
  Pallas kernels: 76.8 us -> 110 us
  local copies, waits for them, and re-layouts: 36.7 us -> 57.4 us
  matrix products: 67.7 us -> 51.1 us
  other arithmetic: 21.8 us -> 36.3 us
    reduce_scatter x3 -> x0, waiting for transfers between devices: 147 us -> none  [the longest x1 81.7 us: body(): lax.psum_scatter(grad_gate_up, 'fsdp', scatter_dimension=0, tiled=True)]
    ppermute x0 -> x53, starting transfers between devices: none -> 77.1 us  [the longest x21 44.9 us: scatter_fsdp(): lax.ppermute(piece, 'fsdp', [(i, (i + step) % size) for i in range(size)])]
    unnamed x10 -> x2, waiting for transfers between devices: 70 us -> 0.03 us
    all_gather x2 -> x0, waiting for transfers between devices: 64.5 us -> none  [the longest x1 37.1 us: body(): down_matrix = lax.all_gather(w_down, 'fsdp', axis=0, tiled=True)]
    ppermute x0 -> x53, waiting for transfers between devices: none -> 64.4 us  [the longest x18 49.3 us: swap(): return lax.ppermute(values, 'ctx', [(i, i ^ bit) for i in range(size)])]
    psum x1 -> x0, waiting for transfers between devices: 32.5 us -> none  [body(): gate_up_sum = lax.psum(gate_up_part, 'ctx').astype(jnp.float32)]
    all_gather x1, waiting for transfers between devices: 44.2 us -> 14.1 us  [body(): attn_every = lax.all_gather(attn_shard, 'fsdp', axis=0, tiled=True)]
    pallas_call x1, Pallas kernels: 43 us -> 59.9 us  [attend_back(): pl.pallas_call(functools.partial(backward_kernel, span), out_shape=(jax.S...]
  transfers between devices with their start and end apart: 9 -> 55, of which waited for: 9 -> 22; matrix products, arithmetic and copies ran while one was open for 15% -> 20% of each run, Pallas kernels for 6% -> 14%
where the time goes in v2:
time: 422 us; the launch traced here: 426 us
  Pallas kernels  110 us (26%)
  waiting for transfers between devices  78.5 us (19%)
  starting transfers between devices  77.2 us (18%)
  local copies, waits for them, and re-layouts  57.4 us (14%)
  matrix products  51.1 us (12%)
  other arithmetic  36.3 us (9%)
  between operations  15.7 us (4%)
    pallas_call x1, Pallas kernels, attend_back(): pl.pallas_call(functools.partial(backward_kernel, span), out_shape=(jax.S...  59.9 us
    pallas_call x1, Pallas kernels, attend(): pl.pallas_call(functools.partial(forward_kernel, span), out_shape=(jax.Sh...  49.9 us
    ppermute x18, waiting for transfers between devices, swap(): return lax.ppermute(values, 'ctx', [(i, i ^ bit) for i in range(size)])  49.3 us
    ppermute x21, starting transfers between devices, scatter_fsdp(): lax.ppermute(piece, 'fsdp', [(i, (i + step) % size) for i in range(size)])  44.9 us
    dot_general x11, matrix products, product(): jnp.einsum(pattern, left_side, right_side, preferred_element_type=jnp.flo...  37.3 us
    ppermute x14, starting transfers between devices, gather_fsdp(): lax.ppermute(values, 'fsdp', [(i, (i + step) % size) for i in range(size)])  23.7 us
    unnamed x103, local copies, waits for them, and re-layouts  14.5 us
    all_gather x1, waiting for transfers between devices, body(): attn_every = lax.all_gather(attn_shard, 'fsdp', axis=0, tiled=True)  14.1 us
  transfers between devices with their start and end apart: 55, of which 22 were waited for; matrix products, arithmetic and copies ran while one was open for 20% of the time, Pallas kernels for 14%

profile of v2, /device:TPU:0, one launch (start us, length us, event | category | flops | bytes accessed | tf_op | source)
XLA Modules:
  0.0 426.1 jit_solution(4012390665761310632)
XLA Ops:
  9.5 3.0 collective-permute-start.9
  17.9 2.6 collective-permute-start.13
  45.8 3.4 collective-permute-start.3
  58.7 3.1 collective-permute-done.4
  65.2 14.1 %all-gather.4.cloned.1.call-done = bf16[576,1664]{1,0:T(8,128)(2,1)} async-done(((bf16[72,1664]{1,0:T(8,128)(2,1)}), bf16[576,1664]{1,0:T(8,128)(2,1)}) %all-gather.4.cloned.1.call-update) | async-done | bytes 1916944 | tf_op jit(solution)/shard_map/all_gather | solution.py:363
  91.3 2.5 copy.74
  98.3 5.2 %fusion.85 = f32[1536,1024]{0,1:T(8,128)} fusion(bf16[1536,576]{1,0:T(8,128)(2,1)S(1)} %bitcast.344, bf16[1024,576]{0,1:T(8,128)(2,1)S(1)} %bitcast.335), kind=kOutput, calls=%fused_computation.266 | convolution fusion | flops 1811939328 | bytes 9240576 | tf_op jit(solution)/shard_map/nd,fd->nf/dot_general | solution.py:44
  115.2 49.9 %attend.1 = (bf16[576,1024]{1,0:T(8,128)(2,1)S(1)}, f32[3,3,1024]{2,1,0:T(4,128)S(1)}) custom-call(s32[8]{0:T(128)S(1)} %get-tuple-element.16.holder_ref, s32[2]{0:T(128)S(1)} %get-tuple-element.65.place_ref, bf16[576,1024]{1,0:T(8,128)(2,1)S(1)} %bitcast.317, bf16[4,2,192,1024]{3,2,1,0:T(8,128)(2,1)S(1)} %bitcast.319), custom_call_target="tpu_custom_call" | custom-call | flops 19327352832 | bytes 4718592 | tf_op jit(solution)/shard_map/attend/pallas_call | solution.py:177
  165.1 2.6 multiply_reduce_fusion.4
  170.0 2.7 fusion.28
  172.7 9.0 %fusion.2 = (bf16[1024,1536]{1,0:T(8,128)(2,1)S(1)}, bf16[1024,1536]{1,0:T(8,128)(2,1)}, bf16[1024,1536]{1,0:T(8,128)(2,1)S(1)}) fusion(f32[1024,1536]{1,0:T(8,128)S(1)} %fusion.28, f32[1536,1024]{0,1:T(8,128)} %fusion.85, bf16[1024,576]{0,1:T(8,128)(2,1)S(1)} %multiply_convert_fusion.1, bf16[576,768]{1,0:T(8,128)(2,1)S(1)} %copy-done.31, ...), kind=kOutput, calls=%fused_computation.3 | convolution fusion | flops 1840644096 | bytes 24969216 | tf_op jit(solution)/shard_map/dot_general | solution.py:52
  183.5 7.9 %convolution_convert_fusion = bf16[576,3072]{1,0:T(8,128)(2,1)} fusion(bf16[1024,576]{0,1:T(8,128)(2,1)S(1)} %multiply_convert_fusion.1, bf16[1024,1536]{1,0:T(8,128)(2,1)} %get-tuple-element.67, bf16[1024,1536]{1,0:T(8,128)(2,1)S(1)} %get-tuple-element.66), kind=kOutput, calls=%fused_computation.11 | convolution fusion | flops 3638231040 | bytes 11010048 | tf_op jit(solution)/shard_map/nd,nf->df/dot_general | solution.py:44
  191.4 7.5 %multiply_reduce_fusion = (bf16[576]{0:T(1024)(128)(2,1)S(1)}, f32[1024]{0:T(1024)S(1)}, f32[1024,576]{0,1:T(8,128)}) fusion(f32[1024,576]{0,1:T(8,128)S(1)} %get-tuple-element.155, f32[1024]{0:T(1024)S(1)} %fusion.73, f32[576]{0:T(1024)S(1)} %get-tuple-element.58, bf16[576,768]{1,0:T(8,128)(2,1)S(1)} %copy-done.29, bf16[576,768]{1,0:T(8,128)(2,1)S(1)} %copy-done.30, ...), kind=kOutput, calls=%fused_computation.45 | convolution fusion | flops 3654154752 | bytes 14560640 | tf_op jit(solution)/shard_map/nf,df->nd/dot_general | solution.py:44
  198.9 3.3 convolution_convert_fusion.1
  202.2 3.9 copy.64
  207.6 3.2 fusion.15
  213.6 59.9 %attend_back.1 = (f32[576,1024]{1,0:T(8,128)S(1)}, bf16[4,2,192,1024]{3,2,1,0:T(8,128)(2,1)S(1)}) custom-call(s32[8]{0:T(128)S(1)} %get-tuple-element.16.holder_ref, s32[2]{0:T(128)S(1)} %get-tuple-element.65.place_ref, bf16[576,1024]{1,0:T(8,128)(2,1)S(1)} %bitcast.318, bf16[576,1024]{1,0:T(8,128)(2,1)S(1)} %convolution_convert_fusion.3.do_ref, ...), custom_call_target="tpu_custom_call" | custom-call | flops 48318382080 | bytes 9437184 | tf_op jit(solution)/shard_map/attend_back/pallas_call | solution.py:207
  280.0 10.2 %collective-permute-done.43 = bf16[8,48,576]{2,1,0:T(8,128)(2,1)S(1)} collective-permute-done((bf16[8,48,576]{2,1,0:T(8,128)(2,1)S(1)}, bf16[8,48,576]{2,1,0:T(8,128)(2,1)S(1)}, u32[]{:S(2)}, u32[]{:S(2)}) %collective-permute-start.43) | collective-permute-done | bytes 442400 | tf_op jit(solution)/shard_map/ppermute | solution.py:237
  292.5 6.9 %collective-permute-start.45 = (bf16[48,576]{1,0:T(8,128)(2,1)S(1)}, bf16[48,576]{1,0:T(8,128)(2,1)S(1)}, u32[]{:S(2)}, u32[]{:S(2)}) collective-permute-start(bf16[48,576]{1,0:T(8,128)(2,1)S(1)} %get-tuple-element.120), channel_id=1, source_target_pairs={{0,8},{4,12},{8,16},{12,20},{16,24},{20,28},{24,0},{28,4},{1,9},{5... | collective-permute-start | bytes 165896 | tf_op jit(solution)/shard_map/ppermute | solution.py:274
  302.6 2.8 collective-permute-start.48
  305.7 2.6 collective-permute-start.49
  320.2 12.1 %collective-permute-done.19 = bf16[2,192,1024]{2,1,0:T(8,128)(2,1)S(1)} collective-permute-done((bf16[2,192,1024]{2,1,0:T(8,128)(2,1)S(1)}, bf16[2,192,1024]{2,1,0:T(8,128)(2,1)S(1)}, u32[]{:S(2)}, u32[]{:S(2)}) %collective-permute-start.19) | collective-permute-done | bytes 786464 | tf_op jit(solution)/shard_map/ppermute | solution.py:237
  335.7 3.0 multiply_reduce_fusion.1
  342.6 4.2 collective-permute-done.32
  355.8 3.1 collective-permute-start.37
  359.5 3.0 collective-permute-done.35
  362.4 6.9 %collective-permute-start.39 = (bf16[72,768]{1,0:T(8,128)(2,1)S(1)}, bf16[72,768]{1,0:T(8,128)(2,1)S(1)}, u32[]{:S(2)}, u32[]{:S(2)}) collective-permute-start(bf16[72,768]{1,0:T(8,128)(2,1)S(1)} %get-tuple-element.98), channel_id=1, source_target_pairs={{0,28},{4,0},{8,4},{12,8},{16,12},{20,16},{24,20},{28,24},{1,29},{... | collective-permute-start | bytes 331784 | tf_op jit(solution)/shard_map/ppermute | solution.py:274
  372.8 3.8 collective-permute-done.40
  381.4 11.6 %collective-permute-done.21 = bf16[576,512]{1,0:T(8,128)(2,1)S(1)} collective-permute-done((bf16[576,512]{1,0:T(8,128)(2,1)S(1)}, bf16[576,512]{1,0:T(8,128)(2,1)S(1)}, u32[]{:S(2)}, u32[]{:S(2)}) %collective-permute-start.21) | collective-permute-done | bytes 589856 | tf_op jit(solution)/shard_map/ppermute | solution.py:237
  395.3 3.5 collective-permute-start.24
  399.7 3.7 collective-permute-start.26
  410.9 3.4 collective-permute-done.29
  (324 shorter events, 145.9 us)
Async XLA Ops:
  7.2 72.1 %all-gather.4.cloned.1.call-start = ((), (), s32[]{:S(2)}) async-start(), calls=%async_computation | async-start | bytes 2156544 | tf_op jit(solution)/shard_map/all_gather | solution.py:363
  9.5 23.5 %collective-permute-start.9 = (bf16[48,576]{1,0:T(8,128)(2,1)}, bf16[48,576]{1,0:T(8,128)(2,1)}, u32[]{:S(2)}, u32[]{:S(2)}) collective-permute-start(bf16[48,576]{1,0:T(8,128)(2,1)} %get-tuple-element.137), channel_id=1, source_target_pairs={{0,4},{4,8},{8,12},{12,16},{16,20},{20,24},{24,28},{28,0},{1,5},{5... | collective-permute-start | bytes 165896 | tf_op jit(solution)/shard_map/ppermute | solution.py:287
  12.5 23.4 %collective-permute-start.10 = (bf16[48,576]{1,0:T(8,128)(2,1)}, bf16[48,576]{1,0:T(8,128)(2,1)}, u32[]{:S(2)}, u32[]{:S(2)}) collective-permute-start(bf16[48,576]{1,0:T(8,128)(2,1)} %get-tuple-element.137), channel_id=1, source_target_pairs={{0,8},{4,12},{8,16},{12,20},{16,24},{20,28},{24,0},{28,4},{1,9},{5... | collective-permute-start | bytes 165896 | tf_op jit(solution)/shard_map/ppermute | solution.py:287
  14.1 24.7 %collective-permute-start.11 = (bf16[48,576]{1,0:T(8,128)(2,1)}, bf16[48,576]{1,0:T(8,128)(2,1)}, u32[]{:S(2)}, u32[]{:S(2)}) collective-permute-start(bf16[48,576]{1,0:T(8,128)(2,1)} %get-tuple-element.137), channel_id=1, source_target_pairs={{0,12},{4,16},{8,20},{12,24},{16,28},{20,0},{24,4},{28,8},{1,13},{... | collective-permute-start | bytes 165896 | tf_op jit(solution)/shard_map/ppermute | solution.py:287
  16.6 24.3 %collective-permute-start.12 = (bf16[48,576]{1,0:T(8,128)(2,1)}, bf16[48,576]{1,0:T(8,128)(2,1)}, u32[]{:S(2)}, u32[]{:S(2)}) collective-permute-start(bf16[48,576]{1,0:T(8,128)(2,1)} %get-tuple-element.137), channel_id=1, source_target_pairs={{0,16},{4,20},{8,24},{12,28},{16,0},{20,4},{24,8},{28,12},{1,17},{... | collective-permute-start | bytes 165896 | tf_op jit(solution)/shard_map/ppermute | solution.py:287
  17.9 25.1 %collective-permute-start.13 = (bf16[48,576]{1,0:T(8,128)(2,1)}, bf16[48,576]{1,0:T(8,128)(2,1)}, u32[]{:S(2)}, u32[]{:S(2)}) collective-permute-start(bf16[48,576]{1,0:T(8,128)(2,1)} %get-tuple-element.137), channel_id=1, source_target_pairs={{0,20},{4,24},{8,28},{12,0},{16,4},{20,8},{24,12},{28,16},{1,21},{... | collective-permute-start | bytes 165896 | tf_op jit(solution)/shard_map/ppermute | solution.py:287
  23.1 90.2 %all-gather.6.cloned.1.call-start = ((), (), s32[]{:S(2)}) async-start(), calls=%async_computation.1 | async-start | bytes 3932160 | tf_op jit(solution)/shard_map/all_gather | solution.py:376
  33.0 12.7 %collective-permute-start.14 = (bf16[48,576]{1,0:T(8,128)(2,1)}, bf16[48,576]{1,0:T(8,128)(2,1)S(1)}, u32[]{:S(2)}, u32[]{:S(2)}) collective-permute-start(bf16[48,576]{1,0:T(8,128)(2,1)} %get-tuple-element.137), channel_id=1, source_target_pairs={{0,24},{4,28},{8,0},{12,4},{16,8},{20,12},{24,16},{28,20},{1,25},{... | collective-permute-start | bytes 165896 | tf_op jit(solution)/shard_map/ppermute | solution.py:287
  35.9 13.9 %collective-permute-start.15 = (bf16[48,576]{1,0:T(8,128)(2,1)}, bf16[48,576]{1,0:T(8,128)(2,1)S(1)}, u32[]{:S(2)}, u32[]{:S(2)}) collective-permute-start(bf16[48,576]{1,0:T(8,128)(2,1)} %get-tuple-element.137), channel_id=1, source_target_pairs={{0,28},{4,0},{8,4},{12,8},{16,12},{20,16},{24,20},{28,24},{1,29},{... | collective-permute-start | bytes 165896 | tf_op jit(solution)/shard_map/ppermute | solution.py:287
  38.8 11.6 %collective-permute-start = (bf16[72,768]{1,0:T(8,128)(2,1)}, bf16[72,768]{1,0:T(8,128)(2,1)S(1)}, u32[]{:S(2)}, u32[]{:S(2)}) collective-permute-start(bf16[72,768]{1,0:T(8,128)(2,1)} %bitcast.359), channel_id=1, source_target_pairs={{0,4},{4,8},{8,12},{12,16},{16,20},{20,24},{24,28},{28,0},{1,5},{5... | collective-permute-start | bytes 331784 | tf_op jit(solution)/shard_map/ppermute | solution.py:287
  40.9 12.6 %collective-permute-start.1 = (bf16[72,768]{1,0:T(8,128)(2,1)}, bf16[72,768]{1,0:T(8,128)(2,1)S(1)}, u32[]{:S(2)}, u32[]{:S(2)}) collective-permute-start(bf16[72,768]{1,0:T(8,128)(2,1)} %bitcast.360), channel_id=1, source_target_pairs={{0,8},{4,12},{8,16},{12,20},{16,24},{20,28},{24,0},{28,4},{1,9},{5... | collective-permute-start | bytes 331784 | tf_op jit(solution)/shard_map/ppermute | solution.py:287
  43.0 13.0 %collective-permute-start.2 = (bf16[72,768]{1,0:T(8,128)(2,1)}, bf16[72,768]{1,0:T(8,128)(2,1)S(1)}, u32[]{:S(2)}, u32[]{:S(2)}) collective-permute-start(bf16[72,768]{1,0:T(8,128)(2,1)} %bitcast.361), channel_id=1, source_target_pairs={{0,12},{4,16},{8,20},{12,24},{16,28},{20,0},{24,4},{28,8},{1,13},{... | collective-permute-start | bytes 331784 | tf_op jit(solution)/shard_map/ppermute | solution.py:287
  45.8 12.3 %collective-permute-start.3 = (bf16[72,768]{1,0:T(8,128)(2,1)}, bf16[72,768]{1,0:T(8,128)(2,1)S(1)}, u32[]{:S(2)}, u32[]{:S(2)}) collective-permute-start(bf16[72,768]{1,0:T(8,128)(2,1)} %bitcast.362), channel_id=1, source_target_pairs={{0,16},{4,20},{8,24},{12,28},{16,0},{20,4},{24,8},{28,12},{1,17},{... | collective-permute-start | bytes 331784 | tf_op jit(solution)/shard_map/ppermute | solution.py:287
  49.8 12.0 %collective-permute-start.4 = (bf16[72,768]{1,0:T(8,128)(2,1)}, bf16[72,768]{1,0:T(8,128)(2,1)S(1)}, u32[]{:S(2)}, u32[]{:S(2)}) collective-permute-start(bf16[72,768]{1,0:T(8,128)(2,1)} %bitcast.363), channel_id=1, source_target_pairs={{0,20},{4,24},{8,28},{12,0},{16,4},{20,8},{24,12},{28,16},{1,21},{... | collective-permute-start | bytes 331784 | tf_op jit(solution)/shard_map/ppermute | solution.py:287
  50.4 12.0 %collective-permute-start.5 = (bf16[72,768]{1,0:T(8,128)(2,1)}, bf16[72,768]{1,0:T(8,128)(2,1)S(1)}, u32[]{:S(2)}, u32[]{:S(2)}) collective-permute-start(bf16[72,768]{1,0:T(8,128)(2,1)} %bitcast.364), channel_id=1, source_target_pairs={{0,24},{4,28},{8,0},{12,4},{16,8},{20,12},{24,16},{28,20},{1,25},{... | collective-permute-start | bytes 331784 | tf_op jit(solution)/shard_map/ppermute | solution.py:287
  55.9 28.2 %collective-permute-start.16 = (bf16[8,48,576]{2,1,0:T(8,128)(2,1)}, bf16[8,48,576]{2,1,0:T(8,128)(2,1)}, u32[]{:S(2)}, u32[]{:S(2)}) collective-permute-start(bf16[8,48,576]{2,1,0:T(8,128)(2,1)} %bitcast_dynamic-update-slice_fusion.7), channel_id=1, source_target_pairs={{0,2},{1,3},{2,0},{3,1},{4,6},{5,7},{6,4},{7,5},{8,10},{9,11},{10,... | collective-permute-start | bytes 1327112 | tf_op jit(solution)/shard_map/ppermute | solution.py:237
  63.8 24.4 %collective-permute-start.7 = (bf16[576,768]{1,0:T(8,128)(2,1)}, bf16[576,768]{1,0:T(8,128)(2,1)}, u32[]{:S(2)}, u32[]{:S(2)}) collective-permute-start(bf16[576,768]{1,0:T(8,128)(2,1)} %bitcast.22), channel_id=1, source_target_pairs={{0,2},{1,3},{2,0},{3,1},{4,6},{5,7},{6,4},{7,5},{8,10},{9,11},{10,... | collective-permute-start | bytes 2654216 | tf_op jit(solution)/shard_map/ppermute | solution.py:237
  91.3 12.2 %collective-permute-start.8 = (bf16[2,576,768]{2,1,0:T(8,128)(2,1)}, bf16[2,576,768]{2,1,0:T(8,128)(2,1)}, u32[]{:S(2)}, u32[]{:S(2)}) collective-permute-start(bf16[2,576,768]{2,1,0:T(8,128)(2,1)} %pad_maximum_fusion.8), channel_id=1, source_target_pairs={{0,1},{1,0},{2,3},{3,2},{4,5},{5,4},{6,7},{7,6},{8,9},{9,8},{10,11... | collective-permute-start | bytes 5308424 | tf_op jit(solution)/shard_map/ppermute | solution.py:237
  207.5 71.4 %collective-permute-start.42 = (bf16[2,8,48,576]{3,2,0,1:T(8,128)(2,1)S(1)}, bf16[2,8,48,576]{3,2,0,1:T(8,128)(2,1)S(1)}, u32[]{:S(2)}, u32[]{:S(2)}) collective-permute-start(bf16[2,8,48,576]{3,2,0,1:T(8,128)(2,1)S(1)} %dynamic-slice_bitcast_fusion.3), channel_id=1, source_target_pairs={{0,1},{1,0},{2,3},{3,2},{4,5},{5,4},{6,7},{7,6},{8,9},{9,8},{10,11... | collective-permute-start | bytes 2654216 | tf_op jit(solution)/shard_map/ppermute | solution.py:237
  273.6 39.3 %collective-permute-start.18 = (bf16[2,2,192,1024]{3,2,1,0:T(8,128)(2,1)S(1)}, bf16[2,2,192,1024]{3,2,1,0:T(8,128)(2,1)S(1)}, u32[]{:S(2)}, u32[]{:S(2)}) collective-permute-start(bf16[2,2,192,1024]{3,2,1,0:T(8,128)(2,1)S(1)} %dynamic-slice_bitcast_fusion.1), channel_id=1, source_target_pairs={{0,1},{1,0},{2,3},{3,2},{4,5},{5,4},{6,7},{7,6},{8,9},{9,8},{10,11... | collective-permute-start | bytes 4718600 | tf_op jit(solution)/shard_map/ppermute | solution.py:237
  279.2 11.0 %collective-permute-start.43 = (bf16[8,48,576]{2,1,0:T(8,128)(2,1)S(1)}, bf16[8,48,576]{2,1,0:T(8,128)(2,1)S(1)}, u32[]{:S(2)}, u32[]{:S(2)}) collective-permute-start(bf16[8,48,576]{2,1,0:T(8,128)(2,1)S(1)} %dynamic-slice_bitcast_fusion.7), channel_id=1, source_target_pairs={{0,2},{1,3},{2,0},{3,1},{4,6},{5,7},{6,4},{7,5},{8,10},{9,11},{10,... | collective-permute-start | bytes 1327112 | tf_op jit(solution)/shard_map/ppermute | solution.py:237
  279.9 38.6 %collective-permute-start.31 = (bf16[2,576,768]{2,1,0:T(8,128)(2,1)S(1)}, bf16[2,576,768]{2,1,0:T(8,128)(2,1)S(1)}, u32[]{:S(2)}, u32[]{:S(2)}) collective-permute-start(bf16[2,576,768]{2,1,0:T(8,128)(2,1)S(1)} %dynamic-slice_bitcast_fusion), channel_id=1, source_target_pairs={{0,1},{1,0},{2,3},{3,2},{4,5},{5,4},{6,7},{7,6},{8,9},{9,8},{10,11... | collective-permute-start | bytes 5308424 | tf_op jit(solution)/shard_map/ppermute | solution.py:237
  313.7 18.6 %collective-permute-start.19 = (bf16[2,192,1024]{2,1,0:T(8,128)(2,1)S(1)}, bf16[2,192,1024]{2,1,0:T(8,128)(2,1)S(1)}, u32[]{:S(2)}, u32[]{:S(2)}) collective-permute-start(bf16[2,192,1024]{2,1,0:T(8,128)(2,1)S(1)} %dynamic-slice_bitcast_fusion.5), channel_id=1, source_target_pairs={{0,2},{1,3},{2,0},{3,1},{4,6},{5,7},{6,4},{7,5},{8,10},{9,11},{10,... | collective-permute-start | bytes 2359304 | tf_op jit(solution)/shard_map/ppermute | solution.py:237
  318.6 33.6 %collective-permute-start.52 = (bf16[2,48,576]{2,1,0:T(8,128)(2,1)}, bf16[2,48,576]{2,1,0:T(8,128)(2,1)}, u32[]{:S(2)}, u32[]{:S(2)}) collective-permute-start(bf16[2,48,576]{2,1,0:T(8,128)(2,1)} %pad_maximum_fusion.20), channel_id=1, source_target_pairs={{0,1},{1,0},{2,3},{3,2},{4,5},{5,4},{6,7},{7,6},{8,9},{9,8},{10,11... | collective-permute-start | bytes 331784 | tf_op jit(solution)/shard_map/ppermute | solution.py:237
  320.2 26.6 %collective-permute-start.32 = (bf16[576,768]{1,0:T(8,128)(2,1)}, bf16[576,768]{1,0:T(8,128)(2,1)}, u32[]{:S(2)}, u32[]{:S(2)}) collective-permute-start(bf16[576,768]{1,0:T(8,128)(2,1)} %dynamic-slice_bitcast_fusion.4), channel_id=1, source_target_pairs={{0,2},{1,3},{2,0},{3,1},{4,6},{5,7},{6,4},{7,5},{8,10},{9,11},{10,... | collective-permute-start | bytes 2654216 | tf_op jit(solution)/shard_map/ppermute | solution.py:237
  342.6 34.2 %collective-permute-start.20 = (bf16[2,576,512]{2,1,0:T(8,128)(2,1)S(1)}, bf16[2,576,512]{2,1,0:T(8,128)(2,1)S(1)}, u32[]{:S(2)}, u32[]{:S(2)}) collective-permute-start(bf16[2,576,512]{2,1,0:T(8,128)(2,1)S(1)} %dynamic-slice_bitcast_fusion.2), channel_id=1, source_target_pairs={{0,1},{1,0},{2,3},{3,2},{4,5},{5,4},{6,7},{7,6},{8,9},{9,8},{10,11... | collective-permute-start | bytes 3538952 | tf_op jit(solution)/shard_map/ppermute | solution.py:237
  351.6 10.8 %collective-permute-start.35 = (bf16[72,768]{1,0:T(8,128)(2,1)S(1)}, bf16[72,768]{1,0:T(8,128)(2,1)S(1)}, u32[]{:S(2)}, u32[]{:S(2)}) collective-permute-start(bf16[72,768]{1,0:T(8,128)(2,1)S(1)} %get-tuple-element.102), channel_id=1, source_target_pairs={{0,12},{4,16},{8,20},{12,24},{16,28},{20,0},{24,4},{28,8},{1,13},{... | collective-permute-start | bytes 331784 | tf_op jit(solution)/shard_map/ppermute | solution.py:274
  353.1 17.1 %collective-permute-start.36 = (bf16[72,768]{1,0:T(8,128)(2,1)S(1)}, bf16[72,768]{1,0:T(8,128)(2,1)S(1)}, u32[]{:S(2)}, u32[]{:S(2)}) collective-permute-start(bf16[72,768]{1,0:T(8,128)(2,1)S(1)} %get-tuple-element.101), channel_id=1, source_target_pairs={{0,16},{4,20},{8,24},{12,28},{16,0},{20,4},{24,8},{28,12},{1,17},{... | collective-permute-start | bytes 331784 | tf_op jit(solution)/shard_map/ppermute | solution.py:274
  355.8 14.4 %collective-permute-start.37 = (bf16[72,768]{1,0:T(8,128)(2,1)S(1)}, bf16[72,768]{1,0:T(8,128)(2,1)S(1)}, u32[]{:S(2)}, u32[]{:S(2)}) collective-permute-start(bf16[72,768]{1,0:T(8,128)(2,1)S(1)} %get-tuple-element.100), channel_id=1, source_target_pairs={{0,20},{4,24},{8,28},{12,0},{16,4},{20,8},{24,12},{28,16},{1,21},{... | collective-permute-start | bytes 331784 | tf_op jit(solution)/shard_map/ppermute | solution.py:274
  358.9 11.3 %collective-permute-start.38 = (bf16[72,768]{1,0:T(8,128)(2,1)S(1)}, bf16[72,768]{1,0:T(8,128)(2,1)S(1)}, u32[]{:S(2)}, u32[]{:S(2)}) collective-permute-start(bf16[72,768]{1,0:T(8,128)(2,1)S(1)} %get-tuple-element.99), channel_id=1, source_target_pairs={{0,24},{4,28},{8,0},{12,4},{16,8},{20,12},{24,16},{28,20},{1,25},{... | collective-permute-start | bytes 331784 | tf_op jit(solution)/shard_map/ppermute | solution.py:274
  377.2 15.8 %collective-permute-start.21 = (bf16[576,512]{1,0:T(8,128)(2,1)S(1)}, bf16[576,512]{1,0:T(8,128)(2,1)S(1)}, u32[]{:S(2)}, u32[]{:S(2)}) collective-permute-start(bf16[576,512]{1,0:T(8,128)(2,1)S(1)} %dynamic-slice_bitcast_fusion.6), channel_id=1, source_target_pairs={{0,2},{1,3},{2,0},{3,1},{4,6},{5,7},{6,4},{7,5},{8,10},{9,11},{10,... | collective-permute-start | bytes 1769480 | tf_op jit(solution)/shard_map/ppermute | solution.py:237
  395.3 11.7 %collective-permute-start.24 = (bf16[72,512]{1,0:T(8,128)(2,1)S(1)}, bf16[72,512]{1,0:T(8,128)(2,1)S(1)}, u32[]{:S(2)}, u32[]{:S(2)}) collective-permute-start(bf16[72,512]{1,0:T(8,128)(2,1)S(1)} %get-tuple-element.112), channel_id=1, source_target_pairs={{0,12},{4,16},{8,20},{12,24},{16,28},{20,0},{24,4},{28,8},{1,13},{... | collective-permute-start | bytes 221192 | tf_op jit(solution)/shard_map/ppermute | solution.py:274
  (72 other events, 688.6 us)
Sparse Core Ops, SparseCore 0:
  23.3 55.9 all-gather.3
  84.2 27.1 all-gather.5

commit v3 on v2

--- a/solution.py
+++ b/solution.py
@@ -100,7 +100,28 @@
             mixed = mixed * shrink + mm(values[held], raised.astype(jnp.bfloat16))
             return new_top, total, mixed
 
-        top, total, mixed = lax.fori_loop(0, place, earlier, (top, total, mixed))
+        def two_earlier(j, carry, query=query):
+            top, total, mixed = carry
+            one, other = holder_ref[2 * j], holder_ref[2 * j + 1]
+            scores_one = mm(keys[one], query)
+            scores_other = mm(keys[other], query)
+            new_top = jnp.maximum(
+                top, jnp.max(jnp.maximum(scores_one, scores_other), axis=0, keepdims=True)
+            )
+            shrink = jnp.exp(top - new_top)
+            raised_one = jnp.exp(scores_one - new_top)
+            raised_other = jnp.exp(scores_other - new_top)
+            total = total * shrink + jnp.sum(raised_one + raised_other, axis=0, keepdims=True)
+            mixed = (
+                mixed * shrink
+                + mm(values[one], raised_one.astype(jnp.bfloat16))
+                + mm(values[other], raised_other.astype(jnp.bfloat16))
+            )
+            return new_top, total, mixed
+
+        paired = place // 2
+        state = lax.fori_loop(0, paired, two_earlier, (top, total, mixed))
+        top, total, mixed = lax.fori_loop(2 * paired, place, earlier, state)
         mixed = mixed / total
         lse = top + jnp.log(total)
         for g in range(GROUP):
@@ -319,14 +340,6 @@
     return jnp.concatenate([every[q] for q in range(4)], axis=1).astype(jnp.float32)
 
 
-def reduce_rows(values):
-    size = lax.axis_size("fsdp")
-    width = values.shape[-1]
-    quarters = jnp.swapaxes(values.reshape(size, 4, -1, width), 0, 1)
-    every = gather_ctx(scatter_fsdp(scatter_ctx(quarters)))
-    return every.reshape(-1, width).astype(jnp.float32)
-
-
 def body(
     tokens,
     cotangent,
@@ -373,7 +386,7 @@
     kv_pre = product(qkv_matrix[:, query_width:], normed, "dh,nd->hn")
     keys_own = rotate(kv_pre[:key_width], cosine, sine_part).astype(jnp.bfloat16)
     kv_own = jnp.stack([keys_own, kv_pre[key_width:].astype(jnp.bfloat16)], axis=0)
-    kv_every = lax.all_gather(kv_own, "ctx", axis=0, tiled=False)
+    kv_every = gather_ctx(kv_own)
     query_pre = product(qkv_matrix[:, :query_width], normed, "dh,nd->hn")
     queries = (rotate(query_pre, cosine, sine_part) * 0.125).astype(jnp.bfloat16)
 
@@ -397,8 +410,23 @@
     grad_normed_two = product(grad_gate_up_pre, gate_up, "nf,df->nd")
     grad_down = product(inner_act, upstream_low, "nf,nd->fd").astype(jnp.bfloat16)
     grad_gate_up = product(normed_two, grad_gate_up_pre, "nd,nf->df").astype(jnp.bfloat16)
-    down_sum = reduce_rows(grad_down)
-    gate_up_sum = reduce_columns(grad_gate_up)
+    grad_down, grad_gate_up, grad_normed_two = lax.optimization_barrier(
+        (grad_down, grad_gate_up, grad_normed_two)
+    )
+    quarters = column_quarters(grad_gate_up)
+    shards = lax.axis_size("fsdp")
+    block = quarters.shape[-1]
+    grad_mlp = jnp.concatenate(
+        [quarters[q].reshape(shards, -1, block) for q in range(4)]
+        + [
+            jnp.pad(
+                grad_down.reshape(shards, -1, model_width),
+                ((0, 0), (0, 0), (0, block - model_width)),
+            )
+        ],
+        axis=1,
+    )
+    mlp_part = lax.psum_scatter(grad_mlp, "fsdp", scatter_dimension=0, tiled=False)
 
     _, second_pull = jax.vjp(rms_norm, middle, gain_two)
     grad_middle_norm, grad_gain_two = second_pull(grad_normed_two)
@@ -409,6 +437,7 @@
     query_grads, kv_grads = attend_back(
         holder, own_spans, queries, grad_attended, attended, lse, kv_every, local_rows
     )
+    kv_grads, mlp_part = lax.optimization_barrier((kv_grads, mlp_part))
     kv_mine = scatter_ctx(kv_grads)
     grad_out = product(attended, middle_low, "hn,nd->hd")
     query_low = (rotate(query_grads, cosine, -sine_part) * 0.125).astype(jnp.bfloat16)
@@ -425,6 +454,10 @@
     )
     attn_grads = jnp.concatenate([grad_qkv, grad_out, grad_gains], axis=1).astype(jnp.bfloat16)
     attn_sum = reduce_columns(attn_grads)
+    mlp_sum = lax.psum(mlp_part, "ctx").astype(jnp.float32)
+    rows = model_width // shards
+    gate_up_sum = jnp.concatenate([mlp_sum[q * rows : (q + 1) * rows] for q in range(4)], axis=1)
+    down_sum = mlp_sum[4 * rows :, :model_width]
     key_start = query_width
     value_start = query_width + key_width
     return (

time: 422 us -> 451 us (1.069); the launches traced: 426 us -> 446 us
  waiting for transfers between devices: 78.5 us -> 131 us
  starting transfers between devices: 77.2 us -> 42.7 us
  other arithmetic: 36.3 us -> 42.6 us
  Pallas kernels: 110 us -> 104 us
    reduce_scatter x0 -> x1, waiting for transfers between devices: none -> 44.9 us  [body(): lax.psum_scatter(grad_mlp, 'fsdp', scatter_dimension=0, tiled=False)]
    ppermute x21 -> x7, starting transfers between devices: 44.9 us -> 12.1 us  [scatter_fsdp(): lax.ppermute(piece, 'fsdp', [(i, (i + step) % size) for i in range(size)])]
    psum x0 -> x1, waiting for transfers between devices: none -> 25.8 us  [body(): mlp_sum = lax.psum(mlp_part, 'ctx').astype(jnp.float32)]
    all_gather x1, waiting for transfers between devices: 14.1 us -> 0.01 us  [body(): attn_every = lax.all_gather(attn_shard, 'fsdp', axis=0, tiled=True)]
    ppermute x21 -> x7, waiting for transfers between devices: 11.7 us -> 1.29 us  [scatter_fsdp(): lax.ppermute(piece, 'fsdp', [(i, (i + step) % size) for i in range(size)])]
    dynamic_update_slice x14, local copies, waits for them, and re-layouts: 13.1 us -> 4.63 us  [gather_fsdp(): every = lax.dynamic_update_index_in_dim(every, came, (me - step) % size, 0)]
    ppermute x14, waiting for transfers between devices: 3.4 us -> 11.6 us  [gather_fsdp(): lax.ppermute(values, 'fsdp', [(i, (i + step) % size) for i in range(size)])]
    pallas_call x1, Pallas kernels: 49.9 us -> 43.6 us  [attend(): pl.pallas_call(functools.partial(forward_kernel, span), out_shape=(jax.Sh...]
  transfers between devices with their start and end apart: 55 -> 36, of which waited for: 22 -> 14; matrix products, arithmetic and copies ran while one was open for 20% -> 16% of each run, Pallas kernels for 14% -> 13%
where the time goes in v3:
time: 451 us; the launch traced here: 446 us
  waiting for transfers between devices  131 us (29%)
  Pallas kernels  104 us (23%)
  local copies, waits for them, and re-layouts  57.1 us (13%)
  matrix products  53.3 us (12%)
  starting transfers between devices  42.7 us (9%)
  other arithmetic  42.6 us (9%)
  between operations  15.4 us (3%)
    pallas_call x1, Pallas kernels, attend_back(): pl.pallas_call(functools.partial(backward_kernel, span), out_shape=(jax.S...  60.1 us
    ppermute x12, waiting for transfers between devices, swap(): return lax.ppermute(values, 'ctx', [(i, i ^ bit) for i in range(size)])  47.1 us
    reduce_scatter x1, waiting for transfers between devices, body(): lax.psum_scatter(grad_mlp, 'fsdp', scatter_dimension=0, tiled=False)  44.9 us
    pallas_call x1, Pallas kernels, attend(): pl.pallas_call(functools.partial(forward_kernel, span), out_shape=(jax.Sh...  43.6 us
    dot_general x11, matrix products, product(): jnp.einsum(pattern, left_side, right_side, preferred_element_type=jnp.flo...  38.8 us
    psum x1, waiting for transfers between devices, body(): mlp_sum = lax.psum(mlp_part, 'ctx').astype(jnp.float32)  25.8 us
    ppermute x14, starting transfers between devices, gather_fsdp(): lax.ppermute(values, 'fsdp', [(i, (i + step) % size) for i in range(size)])  22.9 us
    unnamed x131, local copies, waits for them, and re-layouts  16.5 us
  transfers between devices with their start and end apart: 36, of which 14 were waited for; matrix products, arithmetic and copies ran while one was open for 16% of the time, Pallas kernels for 13%

profile of v3, /device:TPU:0, one launch (start us, length us, event | category | flops | bytes accessed | tf_op | source)
XLA Modules:
  0.0 445.6 jit_solution(18310642607109496931)
XLA Ops:
  8.2 3.0 collective-permute-start.11
  12.8 2.5 collective-permute-start.13
  16.6 2.6 collective-permute-start.15
  34.3 2.7 collective-permute-start.5
  37.1 4.8 %collective-permute-done.2 = bf16[72,768]{1,0:T(8,128)(2,1)S(1)} collective-permute-done((bf16[72,768]{1,0:T(8,128)(2,1)}, bf16[72,768]{1,0:T(8,128)(2,1)S(1)}, u32[]{:S(2)}, u32[]{:S(2)}) %collective-permute-start.2) | collective-permute-done | bytes 110624 | tf_op jit(solution)/shard_map/ppermute | solution.py:308
  43.6 2.7 collective-permute-start.8
  46.9 5.9 %collective-permute-done.4 = bf16[72,768]{1,0:T(8,128)(2,1)S(1)} collective-permute-done((bf16[72,768]{1,0:T(8,128)(2,1)}, bf16[72,768]{1,0:T(8,128)(2,1)S(1)}, u32[]{:S(2)}, u32[]{:S(2)}) %collective-permute-start.4) | collective-permute-done | bytes 110624 | tf_op jit(solution)/shard_map/ppermute | solution.py:308
  58.1 8.7 %collective-permute-done.18 = bf16[8,48,576]{2,1,0:T(8,128)(2,1)S(1)} collective-permute-done((bf16[8,48,576]{2,1,0:T(8,128)(2,1)S(1)}, bf16[8,48,576]{2,1,0:T(8,128)(2,1)S(1)}, u32[]{:S(2)}, u32[]{:S(2)}) %collective-permute-start.18) | collective-permute-done | bytes 442400 | tf_op jit(solution)/shard_map/ppermute | solution.py:258
  76.7 4.1 collective-permute-done.9
  92.9 5.3 %fusion.68 = f32[1536,1024]{0,1:T(8,128)} fusion(bf16[1536,576]{1,0:T(8,128)(2,1)S(1)} %bitcast.258, bf16[1024,576]{0,1:T(8,128)(2,1)S(1)} %bitcast.246), kind=kOutput, calls=%fused_computation.216 | convolution fusion | flops 1811939328 | bytes 9240576 | tf_op jit(solution)/shard_map/nd,fd->nf/dot_general | solution.py:44
  100.3 10.6 %collective-permute-done = bf16[2,192,1024]{2,1,0:T(8,128)(2,1)S(1)} collective-permute-done((bf16[2,192,1024]{2,1,0:T(8,128)(2,1)S(1)}, bf16[2,192,1024]{2,1,0:T(8,128)(2,1)S(1)}, u32[]{:S(2)}, u32[]{:S(2)}) %collective-permute-start) | collective-permute-done | bytes 786464 | tf_op jit(solution)/shard_map/ppermute | solution.py:258
  125.1 43.6 %attend.1 = (bf16[576,1024]{1,0:T(8,128)(2,1)S(1)}, f32[3,3,1024]{2,1,0:T(4,128)S(1)}) custom-call(s32[8]{0:T(128)S(1)} %get-tuple-element.21.holder_ref, s32[2]{0:T(128)S(1)} %get-tuple-element.75.place_ref, bf16[576,1024]{1,0:T(8,128)(2,1)S(1)} %bitcast.234, bf16[4,2,192,1024]{3,2,1,0:T(8,128)(2,1)S(1)} %bitcast.229), custom_call_target="tpu_custom_call" | custom-call | flops 19327352832 | bytes 4718592 | tf_op jit(solution)/shard_map/attend/pallas_call | solution.py:198
  168.7 3.0 multiply_reduce_fusion.4
  174.0 2.6 fusion.26
  176.7 7.8 %fusion.2 = (bf16[1024,1536]{1,0:T(8,128)(2,1)}, bf16[1024,1536]{1,0:T(8,128)(2,1)}, bf16[1024,1536]{1,0:T(8,128)(2,1)}) fusion(f32[1024,1536]{1,0:T(8,128)S(1)} %fusion.26, f32[1536,1024]{0,1:T(8,128)S(1)} %bitcast.279, bf16[1024,576]{0,1:T(8,128)(2,1)S(1)} %multiply_convert_fusion.1, bf16[576,768]{1,0:T(8,128)(2,1)S(1)} %copy-done.47, ...), kind=kOutput, calls=%fused_computation.3 | convolution fusion | flops 1840644096 | bytes 24969216 | tf_op jit(solution)/shard_map/dot_general | solution.py:52
  184.6 8.2 %fusion.5 = f32[1024,576]{0,1:T(8,128)} fusion(bf16[1024,1536]{1,0:T(8,128)(2,1)} %get-tuple-element.77, bf16[1024,1536]{1,0:T(8,128)(2,1)} %get-tuple-element.76, bf16[576,768]{1,0:T(8,128)(2,1)S(1)} %copy-done.45, bf16[576,768]{1,0:T(8,128)(2,1)S(1)} %copy-done.46, bf16[576,768]{1,0:T(8,128)(2,1)S(1)} %copy-done.47, bf16[576,768]{1,0:T(8,128)(2,1)S(1)} %copy-done.44), kind=kOutput, calls=%fused_computation.12 | convolution fusion | flops 3650617344 | bytes 12189696 | tf_op jit(solution)/shard_map/nf,df->nd/dot_general | solution.py:44
  192.8 4.4 convolution_convert_fusion
  197.2 3.2 convolution_convert_fusion.1
  203.0 3.9 copy.59
  213.0 3.2 multiply_reduce_fusion
  218.7 3.2 convolution_convert_fusion.3.do_ref
  221.9 60.1 %attend_back.1 = (f32[576,1024]{1,0:T(8,128)S(1)}, bf16[4,2,192,1024]{3,2,1,0:T(8,128)(2,1)S(1)}) custom-call(s32[8]{0:T(128)S(1)} %get-tuple-element.21.holder_ref, s32[2]{0:T(128)S(1)} %get-tuple-element.75.place_ref, bf16[576,1024]{1,0:T(8,128)(2,1)S(1)} %bitcast.235, bf16[576,1024]{1,0:T(8,128)(2,1)S(1)} %convolution_convert_fusion.3.do_ref, ...), custom_call_target="tpu_custom_call" | custom-call | flops 48318382080 | bytes 9437184 | tf_op jit(solution)/shard_map/attend_back/pallas_call | solution.py:228
  285.2 44.9 %reduce-scatter.2.cloned.1.call-done = bf16[1,480,768]{2,1,0:T(8,128)(2,1)} async-done(((bf16[8,480,768]{2,1,0:T(8,128)(2,1)}), bf16[1,480,768]{2,1,0:T(8,128)(2,1)}) %reduce-scatter.2.cloned.1.call-update) | async-done | bytes 737296 | tf_op jit(solution)/shard_map/reduce_scatter | solution.py:429
  330.2 2.9 dynamic-slice_bitcast_fusion
  333.1 3.7 collective-permute-done.20
  345.0 13.6 %collective-permute-done.21 = bf16[2,192,1024]{2,1,0:T(8,128)(2,1)S(1)} collective-permute-done((bf16[2,192,1024]{2,1,0:T(8,128)(2,1)S(1)}, bf16[2,192,1024]{2,1,0:T(8,128)(2,1)S(1)}, u32[]{:S(2)}, u32[]{:S(2)}) %collective-permute-start.21) | collective-permute-done | bytes 786464 | tf_op jit(solution)/shard_map/ppermute | solution.py:258
  362.1 3.6 multiply_reduce_fusion.1
  372.4 2.8 collective-permute-done.22
  379.5 3.9 add_convert_fusion
  384.5 25.8 %all-reduce.5.cloned.1.call-done = bf16[480,768]{1,0:T(8,128)(2,1)} async-done(((bf16[480,768]{1,0:T(8,128)(2,1)}), bf16[480,768]{1,0:T(8,128)(2,1)}) %all-reduce.5.cloned.1.call-update) | async-done | bytes 737296 | tf_op jit(solution)/shard_map/psum | solution.py:457
  420.5 2.4 collective-permute-start.28
  429.6 3.6 collective-permute-done.31
  (302 shorter events, 126.8 us)
Async XLA Ops:
  7.2 80.3 %all-gather.2.cloned.1.call-start = ((), (), s32[]{:S(2)}) async-start(), calls=%async_computation.1 | async-start | bytes 2156544 | tf_op jit(solution)/shard_map/all_gather | solution.py:376
  8.2 19.6 %collective-permute-start.11 = (bf16[48,576]{1,0:T(8,128)(2,1)S(1)}, bf16[48,576]{1,0:T(8,128)(2,1)S(1)}, u32[]{:S(2)}, u32[]{:S(2)}) collective-permute-start(bf16[48,576]{1,0:T(8,128)(2,1)S(1)} %get-tuple-element.131), channel_id=1, source_target_pairs={{0,4},{4,8},{8,12},{12,16},{16,20},{20,24},{24,28},{28,0},{1,5},{5... | collective-permute-start | bytes 165896 | tf_op jit(solution)/shard_map/ppermute | solution.py:308
  11.2 18.0 %collective-permute-start.12 = (bf16[48,576]{1,0:T(8,128)(2,1)S(1)}, bf16[48,576]{1,0:T(8,128)(2,1)S(1)}, u32[]{:S(2)}, u32[]{:S(2)}) collective-permute-start(bf16[48,576]{1,0:T(8,128)(2,1)S(1)} %get-tuple-element.131), channel_id=1, source_target_pairs={{0,8},{4,12},{8,16},{12,20},{16,24},{20,28},{24,0},{28,4},{1,9},{5... | collective-permute-start | bytes 165896 | tf_op jit(solution)/shard_map/ppermute | solution.py:308
  12.8 17.9 %collective-permute-start.13 = (bf16[48,576]{1,0:T(8,128)(2,1)S(1)}, bf16[48,576]{1,0:T(8,128)(2,1)S(1)}, u32[]{:S(2)}, u32[]{:S(2)}) collective-permute-start(bf16[48,576]{1,0:T(8,128)(2,1)S(1)} %get-tuple-element.131), channel_id=1, source_target_pairs={{0,12},{4,16},{8,20},{12,24},{16,28},{20,0},{24,4},{28,8},{1,13},{... | collective-permute-start | bytes 165896 | tf_op jit(solution)/shard_map/ppermute | solution.py:308
  15.3 16.0 %collective-permute-start.14 = (bf16[48,576]{1,0:T(8,128)(2,1)S(1)}, bf16[48,576]{1,0:T(8,128)(2,1)S(1)}, u32[]{:S(2)}, u32[]{:S(2)}) collective-permute-start(bf16[48,576]{1,0:T(8,128)(2,1)S(1)} %get-tuple-element.131), channel_id=1, source_target_pairs={{0,16},{4,20},{8,24},{12,28},{16,0},{20,4},{24,8},{28,12},{1,17},{... | collective-permute-start | bytes 165896 | tf_op jit(solution)/shard_map/ppermute | solution.py:308
  16.6 15.6 %collective-permute-start.15 = (bf16[48,576]{1,0:T(8,128)(2,1)S(1)}, bf16[48,576]{1,0:T(8,128)(2,1)S(1)}, u32[]{:S(2)}, u32[]{:S(2)}) collective-permute-start(bf16[48,576]{1,0:T(8,128)(2,1)S(1)} %get-tuple-element.131), channel_id=1, source_target_pairs={{0,20},{4,24},{8,28},{12,0},{16,4},{20,8},{24,12},{28,16},{1,21},{... | collective-permute-start | bytes 165896 | tf_op jit(solution)/shard_map/ppermute | solution.py:308
  21.9 308.3 %reduce-scatter.2.cloned.1.call-start = ((), (), s32[]{:S(2)}) async-start(), calls=%async_computation.2 | async-start | bytes 6635520 | tf_op jit(solution)/shard_map/reduce_scatter | solution.py:429
  27.8 6.4 %collective-permute-start.16 = (bf16[48,576]{1,0:T(8,128)(2,1)S(1)}, bf16[48,576]{1,0:T(8,128)(2,1)S(1)}, u32[]{:S(2)}, u32[]{:S(2)}) collective-permute-start(bf16[48,576]{1,0:T(8,128)(2,1)S(1)} %get-tuple-element.131), channel_id=1, source_target_pairs={{0,24},{4,28},{8,0},{12,4},{16,8},{20,12},{24,16},{28,20},{1,25},{... | collective-permute-start | bytes 165896 | tf_op jit(solution)/shard_map/ppermute | solution.py:308
  29.2 7.8 %collective-permute-start.17 = (bf16[48,576]{1,0:T(8,128)(2,1)S(1)}, bf16[48,576]{1,0:T(8,128)(2,1)S(1)}, u32[]{:S(2)}, u32[]{:S(2)}) collective-permute-start(bf16[48,576]{1,0:T(8,128)(2,1)S(1)} %get-tuple-element.131), channel_id=1, source_target_pairs={{0,28},{4,0},{8,4},{12,8},{16,12},{20,16},{24,20},{28,24},{1,29},{... | collective-permute-start | bytes 165896 | tf_op jit(solution)/shard_map/ppermute | solution.py:308
  30.7 11.2 %collective-permute-start.2 = (bf16[72,768]{1,0:T(8,128)(2,1)}, bf16[72,768]{1,0:T(8,128)(2,1)S(1)}, u32[]{:S(2)}, u32[]{:S(2)}) collective-permute-start(bf16[72,768]{1,0:T(8,128)(2,1)} %bitcast.19), channel_id=1, source_target_pairs={{0,4},{4,8},{8,12},{12,16},{16,20},{20,24},{24,28},{28,0},{1,5},{5... | collective-permute-start | bytes 331784 | tf_op jit(solution)/shard_map/ppermute | solution.py:308
  31.4 12.2 %collective-permute-start.3 = (bf16[72,768]{1,0:T(8,128)(2,1)}, bf16[72,768]{1,0:T(8,128)(2,1)S(1)}, u32[]{:S(2)}, u32[]{:S(2)}) collective-permute-start(bf16[72,768]{1,0:T(8,128)(2,1)} %bitcast.19), channel_id=1, source_target_pairs={{0,8},{4,12},{8,16},{12,20},{16,24},{20,28},{24,0},{28,4},{1,9},{5... | collective-permute-start | bytes 331784 | tf_op jit(solution)/shard_map/ppermute | solution.py:308
  32.1 20.7 %collective-permute-start.4 = (bf16[72,768]{1,0:T(8,128)(2,1)}, bf16[72,768]{1,0:T(8,128)(2,1)S(1)}, u32[]{:S(2)}, u32[]{:S(2)}) collective-permute-start(bf16[72,768]{1,0:T(8,128)(2,1)} %bitcast.19), channel_id=1, source_target_pairs={{0,12},{4,16},{8,20},{12,24},{16,28},{20,0},{24,4},{28,8},{1,13},{... | collective-permute-start | bytes 331784 | tf_op jit(solution)/shard_map/ppermute | solution.py:308
  34.3 20.7 %collective-permute-start.5 = (bf16[72,768]{1,0:T(8,128)(2,1)}, bf16[72,768]{1,0:T(8,128)(2,1)S(1)}, u32[]{:S(2)}, u32[]{:S(2)}) collective-permute-start(bf16[72,768]{1,0:T(8,128)(2,1)} %bitcast.19), channel_id=1, source_target_pairs={{0,16},{4,20},{8,24},{12,28},{16,0},{20,4},{24,8},{28,12},{1,17},{... | collective-permute-start | bytes 331784 | tf_op jit(solution)/shard_map/ppermute | solution.py:308
  37.0 18.6 %collective-permute-start.6 = (bf16[72,768]{1,0:T(8,128)(2,1)}, bf16[72,768]{1,0:T(8,128)(2,1)S(1)}, u32[]{:S(2)}, u32[]{:S(2)}) collective-permute-start(bf16[72,768]{1,0:T(8,128)(2,1)} %bitcast.19), channel_id=1, source_target_pairs={{0,20},{4,24},{8,28},{12,0},{16,4},{20,8},{24,12},{28,16},{1,21},{... | collective-permute-start | bytes 331784 | tf_op jit(solution)/shard_map/ppermute | solution.py:308
  41.9 14.4 %collective-permute-start.7 = (bf16[72,768]{1,0:T(8,128)(2,1)}, bf16[72,768]{1,0:T(8,128)(2,1)S(1)}, u32[]{:S(2)}, u32[]{:S(2)}) collective-permute-start(bf16[72,768]{1,0:T(8,128)(2,1)} %bitcast.19), channel_id=1, source_target_pairs={{0,24},{4,28},{8,0},{12,4},{16,8},{20,12},{24,16},{28,20},{1,25},{... | collective-permute-start | bytes 331784 | tf_op jit(solution)/shard_map/ppermute | solution.py:308
  43.6 13.3 %collective-permute-start.8 = (bf16[72,768]{1,0:T(8,128)(2,1)}, bf16[72,768]{1,0:T(8,128)(2,1)S(1)}, u32[]{:S(2)}, u32[]{:S(2)}) collective-permute-start(bf16[72,768]{1,0:T(8,128)(2,1)} %bitcast.19), channel_id=1, source_target_pairs={{0,28},{4,0},{8,4},{12,8},{16,12},{20,16},{24,20},{28,24},{1,29},{... | collective-permute-start | bytes 331784 | tf_op jit(solution)/shard_map/ppermute | solution.py:308
  52.8 14.0 %collective-permute-start.18 = (bf16[8,48,576]{2,1,0:T(8,128)(2,1)S(1)}, bf16[8,48,576]{2,1,0:T(8,128)(2,1)S(1)}, u32[]{:S(2)}, u32[]{:S(2)}) collective-permute-start(bf16[8,48,576]{2,1,0:T(8,128)(2,1)S(1)} %bitcast_dynamic-update-slice_fusion.7), channel_id=1, source_target_pairs={{0,2},{1,3},{2,0},{3,1},{4,6},{5,7},{6,4},{7,5},{8,10},{9,11},{10,... | collective-permute-start | bytes 1327112 | tf_op jit(solution)/shard_map/ppermute | solution.py:258
  57.6 23.2 %collective-permute-start.9 = (bf16[576,768]{1,0:T(8,128)(2,1)}, bf16[576,768]{1,0:T(8,128)(2,1)}, u32[]{:S(2)}, u32[]{:S(2)}) collective-permute-start(bf16[576,768]{1,0:T(8,128)(2,1)} %bitcast.27), channel_id=1, source_target_pairs={{0,2},{1,3},{2,0},{3,1},{4,6},{5,7},{6,4},{7,5},{8,10},{9,11},{10,... | collective-permute-start | bytes 2654216 | tf_op jit(solution)/shard_map/ppermute | solution.py:258
  68.8 14.9 %collective-permute-start.19 = (bf16[2,8,48,576]{3,2,1,0:T(8,128)(2,1)}, bf16[2,8,48,576]{3,2,1,0:T(8,128)(2,1)}, u32[]{:S(2)}, u32[]{:S(2)}) collective-permute-start(bf16[2,8,48,576]{3,2,1,0:T(8,128)(2,1)} %pad_maximum_fusion.9), channel_id=1, source_target_pairs={{0,1},{1,0},{2,3},{3,2},{4,5},{5,4},{6,7},{7,6},{8,9},{9,8},{10,11... | collective-permute-start | bytes 2654216 | tf_op jit(solution)/shard_map/ppermute | solution.py:258
  83.7 14.5 %collective-permute-start.10 = (bf16[2,576,768]{2,1,0:T(8,128)(2,1)}, bf16[2,576,768]{2,1,0:T(8,128)(2,1)}, u32[]{:S(2)}, u32[]{:S(2)}) collective-permute-start(bf16[2,576,768]{2,1,0:T(8,128)(2,1)} %pad_maximum_fusion.7), channel_id=1, source_target_pairs={{0,1},{1,0},{2,3},{3,2},{4,5},{5,4},{6,7},{7,6},{8,9},{9,8},{10,11... | collective-permute-start | bytes 5308424 | tf_op jit(solution)/shard_map/ppermute | solution.py:258
  91.4 19.5 %collective-permute-start = (bf16[2,192,1024]{2,1,0:T(8,128)(2,1)S(1)}, bf16[2,192,1024]{2,1,0:T(8,128)(2,1)S(1)}, u32[]{:S(2)}, u32[]{:S(2)}) collective-permute-start(bf16[2,192,1024]{2,1,0:T(8,128)(2,1)S(1)} %pad_maximum_fusion.12), channel_id=1, source_target_pairs={{0,2},{1,3},{2,0},{3,1},{4,6},{5,7},{6,4},{7,5},{8,10},{9,11},{10,... | collective-permute-start | bytes 2359304 | tf_op jit(solution)/shard_map/ppermute | solution.py:258
  112.3 10.0 %collective-permute-start.1 = (bf16[2,2,192,1024]{3,2,1,0:T(8,128)(2,1)}, bf16[2,2,192,1024]{3,2,1,0:T(8,128)(2,1)}, u32[]{:S(2)}, u32[]{:S(2)}) collective-permute-start(bf16[2,2,192,1024]{3,2,1,0:T(8,128)(2,1)} %pad_maximum_fusion.8), channel_id=1, source_target_pairs={{0,1},{1,0},{2,3},{3,2},{4,5},{5,4},{6,7},{7,6},{8,9},{9,8},{10,11... | collective-permute-start | bytes 4718600 | tf_op jit(solution)/shard_map/ppermute | solution.py:258
  212.9 197.4 %all-reduce.5.cloned.1.call-start = ((), (), s32[]{:S(2)}) async-start(), calls=%async_computation.3 | async-start | bytes 1474560 | tf_op jit(solution)/shard_map/psum | solution.py:457
  339.0 19.6 %collective-permute-start.21 = (bf16[2,192,1024]{2,1,0:T(8,128)(2,1)S(1)}, bf16[2,192,1024]{2,1,0:T(8,128)(2,1)S(1)}, u32[]{:S(2)}, u32[]{:S(2)}) collective-permute-start(bf16[2,192,1024]{2,1,0:T(8,128)(2,1)S(1)} %dynamic-slice_bitcast_fusion.2), channel_id=1, source_target_pairs={{0,2},{1,3},{2,0},{3,1},{4,6},{5,7},{6,4},{7,5},{8,10},{9,11},{10,... | collective-permute-start | bytes 2359304 | tf_op jit(solution)/shard_map/ppermute | solution.py:258
  378.0 33.4 %collective-permute-start.23 = (bf16[576,512]{1,0:T(8,128)(2,1)}, bf16[576,512]{1,0:T(8,128)(2,1)}, u32[]{:S(2)}, u32[]{:S(2)}) collective-permute-start(bf16[576,512]{1,0:T(8,128)(2,1)} %dynamic-slice_bitcast_fusion.3), channel_id=1, source_target_pairs={{0,2},{1,3},{2,0},{3,1},{4,6},{5,7},{6,4},{7,5},{8,10},{9,11},{10,... | collective-permute-start | bytes 1769480 | tf_op jit(solution)/shard_map/ppermute | solution.py:258
  412.9 10.0 %collective-permute-start.24 = (bf16[72,512]{1,0:T(8,128)(2,1)S(1)}, bf16[72,512]{1,0:T(8,128)(2,1)S(1)}, u32[]{:S(2)}, u32[]{:S(2)}) collective-permute-start(bf16[72,512]{1,0:T(8,128)(2,1)S(1)} %get-tuple-element.116), channel_id=1, source_target_pairs={{0,4},{4,8},{8,12},{12,16},{16,20},{20,24},{24,28},{28,0},{1,5},{5... | collective-permute-start | bytes 221192 | tf_op jit(solution)/shard_map/ppermute | solution.py:295
  414.4 10.0 %collective-permute-start.25 = (bf16[72,512]{1,0:T(8,128)(2,1)S(1)}, bf16[72,512]{1,0:T(8,128)(2,1)S(1)}, u32[]{:S(2)}, u32[]{:S(2)}) collective-permute-start(bf16[72,512]{1,0:T(8,128)(2,1)S(1)} %get-tuple-element.122), channel_id=1, source_target_pairs={{0,8},{4,12},{8,16},{12,20},{16,24},{20,28},{24,0},{28,4},{1,9},{5... | collective-permute-start | bytes 221192 | tf_op jit(solution)/shard_map/ppermute | solution.py:295
  416.7 10.7 %collective-permute-start.26 = (bf16[72,512]{1,0:T(8,128)(2,1)S(1)}, bf16[72,512]{1,0:T(8,128)(2,1)S(1)}, u32[]{:S(2)}, u32[]{:S(2)}) collective-permute-start(bf16[72,512]{1,0:T(8,128)(2,1)S(1)} %get-tuple-element.121), channel_id=1, source_target_pairs={{0,12},{4,16},{8,20},{12,24},{16,28},{20,0},{24,4},{28,8},{1,13},{... | collective-permute-start | bytes 221192 | tf_op jit(solution)/shard_map/ppermute | solution.py:295
  419.1 8.8 %collective-permute-start.27 = (bf16[72,512]{1,0:T(8,128)(2,1)S(1)}, bf16[72,512]{1,0:T(8,128)(2,1)S(1)}, u32[]{:S(2)}, u32[]{:S(2)}) collective-permute-start(bf16[72,512]{1,0:T(8,128)(2,1)S(1)} %get-tuple-element.120), channel_id=1, source_target_pairs={{0,16},{4,20},{8,24},{12,28},{16,0},{20,4},{24,8},{28,12},{1,17},{... | collective-permute-start | bytes 221192 | tf_op jit(solution)/shard_map/ppermute | solution.py:295
  420.5 7.4 %collective-permute-start.28 = (bf16[72,512]{1,0:T(8,128)(2,1)S(1)}, bf16[72,512]{1,0:T(8,128)(2,1)S(1)}, u32[]{:S(2)}, u32[]{:S(2)}) collective-permute-start(bf16[72,512]{1,0:T(8,128)(2,1)S(1)} %get-tuple-element.119), channel_id=1, source_target_pairs={{0,20},{4,24},{8,28},{12,0},{16,4},{20,8},{24,12},{28,16},{1,21},{... | collective-permute-start | bytes 221192 | tf_op jit(solution)/shard_map/ppermute | solution.py:295
  422.9 5.0 %collective-permute-start.29 = (bf16[72,512]{1,0:T(8,128)(2,1)S(1)}, bf16[72,512]{1,0:T(8,128)(2,1)S(1)}, u32[]{:S(2)}, u32[]{:S(2)}) collective-permute-start(bf16[72,512]{1,0:T(8,128)(2,1)S(1)} %get-tuple-element.118), channel_id=1, source_target_pairs={{0,24},{4,28},{8,0},{12,4},{16,8},{20,12},{24,16},{28,20},{1,25},{... | collective-permute-start | bytes 221192 | tf_op jit(solution)/shard_map/ppermute | solution.py:295
  428.8 4.4 collective-permute-start.31
  (65 other events, 364.8 us)
Sparse Core Ops, SparseCore 0:
  22.0 54.6 all-gather.1
  213.1 117.0 reduce-scatter.1
  372.5 37.7 all-reduce.4
